TPU v7x, 256 devices: a whole 4x4x8 slice. The times are simulated.
256 devices in a mesh: node: 16 (over x, y), local: 8 (over z), replica: 2 (over core).
Axes of the slice: x: 4, y: 4, z: 8, core: 2. Of those that a mesh axis runs over, the one named last changes fastest.
Arguments:
- out_grad: bfloat16 [32768, 3584], P(('node', 'local', 'replica')), may hold values from -6 to 6
- expert_ids: int32 [32768, 8], P(('node', 'local', 'replica')), may hold values from 0 to 127, as said below
- drop_flags: int32 [32768, 8], P(('node', 'local', 'replica')), may hold values from 0 to 1, as said below
- router_logits: float32 [32768, 8], P(('node', 'local', 'replica')), may hold values from -4 to 4
- saved_hidden: bfloat16 [2, 128, 768, 1024], P('replica', ('node', 'local')), may hold values from -1.1953125 to 1.1953125
- down_weight: bfloat16 [128, 3584, 1024], P(('node', 'local'), 'replica'), may hold values from -0.09375 to 0.09375
Outputs:
- grad_logits: float32 [32768, 8], P(('node', 'local', 'replica'))
- grad_hidden: bfloat16 [2, 128, 768, 1024], P('replica', ('node', 'local'))
- grad_down: bfloat16 [128, 3584, 1024], P(('node', 'local'), 'replica')
Inputs may be any that keep to these rules, and one draw needn't show every extreme that they name: `expert_ids`: each row names 8 different experts, all from at most 4 groups of 8 consecutive experts. `drop_flags`: among the kept pairs of one device's 128 rows, at most 6 name the same expert; in every draw some expert gets exactly 6 kept pairs from every device's rows.
All inputs are finite; a program needn't handle non-finite values.
Results may differ from a plain program's by a relative error of at most 0.0057.
Values may be sent and summed in bfloat16 or wider, within the bound.
No kernel may reach another device: no remote copies, remote signals or barrier semaphores. Data moves between devices by JAX's collectives and lax.ppermute only.
A program may use at most 128 MiB of HBM per device.

v0:
```python
import jax
import jax.numpy as jnp
from jax import lax
from jax.sharding import PartitionSpec as P

route_scale = 2.5


def pair_slots(expert_ids, drop_flags, experts, capacity):
    pair_ids = expert_ids.reshape(-1)
    kept_pair = (1 - drop_flags).reshape(-1)
    expert_row = jnp.arange(experts, dtype=jnp.int32)
    onehot = (pair_ids[:, None] == expert_row[None, :]).astype(jnp.int32) * kept_pair[:, None]
    before = jnp.cumsum(onehot, axis=0) - onehot
    pair_rank = jnp.sum(before * onehot, axis=1)
    return jnp.where(kept_pair > 0, pair_ids * capacity + pair_rank, -1)


def local(out_grad, expert_ids, drop_flags, router_logits, saved_hidden, down_weight):
    groups = lax.axis_size("node")
    members = lax.axis_size("local")
    experts = groups * members
    slot_total = saved_hidden.shape[2]
    capacity = slot_total // experts
    tok_rows = out_grad.shape[0]
    top_count = expert_ids.shape[1]
    width = out_grad.shape[1]
    hidden_units = saved_hidden.shape[3]
    slot_ids = pair_slots(expert_ids, drop_flags, experts, capacity)
    affinity = jax.nn.sigmoid(router_logits)
    denominator = jnp.sum(affinity, axis=1, keepdims=True)
    gate_sent = (route_scale * affinity / denominator).astype(jnp.bfloat16)
    slot_range = jnp.arange(slot_total, dtype=jnp.int32)
    match = slot_ids[None, :] == slot_range[:, None]
    owner = jnp.any(match.reshape(slot_total, tok_rows, top_count), axis=2).astype(jnp.bfloat16)
    send_rows = jnp.dot(owner, out_grad, preferred_element_type=jnp.float32).astype(jnp.bfloat16)
    send_gate = jnp.sum(
        jnp.where(match, gate_sent.reshape(-1).astype(jnp.float32)[None, :], 0.0), axis=1
    ).astype(jnp.bfloat16)
    got_rows, got_gate = (
        lax.all_to_all(
            send_rows.reshape(experts, capacity, width),
            ("node", "local"),
            split_axis=0,
            concat_axis=0,
            tiled=True,
        ),
        lax.all_to_all(
            send_gate.reshape(experts, capacity),
            ("node", "local"),
            split_axis=0,
            concat_axis=0,
            tiled=True,
        ),
    )
    got_rows = got_rows.reshape(slot_total, width)
    slot_gate = got_gate.reshape(slot_total).astype(jnp.float32)
    hidden = saved_hidden.reshape(slot_total, hidden_units)
    weight_local = down_weight.reshape(down_weight.shape[1], hidden_units)
    columns = got_rows
    backward = jnp.dot(
        columns,
        lax.all_gather(weight_local, "replica", axis=0, tiled=True),
        preferred_element_type=jnp.float32,
    )
    grad_hidden = (slot_gate[:, None] * backward).astype(jnp.bfloat16).reshape(saved_hidden.shape)
    gate_grad = jnp.sum(hidden.astype(jnp.float32) * backward, axis=1)
    scaled = (slot_gate[:, None] * got_rows.astype(jnp.float32)).astype(jnp.bfloat16)
    columns = scaled
    summed = lax.psum_scatter(
        lax.dot_general(
            columns, hidden, (((0,), (0,)), ((), ())), preferred_element_type=jnp.float32
        ),
        "replica",
        scatter_dimension=0,
        tiled=True,
    )
    grad_down = summed.astype(jnp.bfloat16).reshape(down_weight.shape)
    returned = lax.all_to_all(
        gate_grad.reshape(experts, capacity),
        ("node", "local"),
        split_axis=0,
        concat_axis=0,
        tiled=True,
    )
    returned = returned.reshape(-1)
    safe_index = jnp.maximum(slot_ids, 0)
    pair_grad = jnp.where(slot_ids >= 0, returned[safe_index], 0.0).reshape(tok_rows, top_count)
    weighted = jnp.sum(pair_grad * affinity, axis=1, keepdims=True)
    grad_affinity = route_scale * (pair_grad / denominator - weighted / (denominator * denominator))
    grad_logits = grad_affinity * affinity * (1.0 - affinity)
    return (grad_logits, grad_hidden, grad_down)


def solution(mesh):
    return jax.shard_map(
        local,
        mesh=mesh,
        in_specs=(
            P(("node", "local", "replica"), None),
            P(("node", "local", "replica"), None),
            P(("node", "local", "replica"), None),
            P(("node", "local", "replica"), None),
            P("replica", ("node", "local"), None, None),
            P(("node", "local"), "replica", None),
        ),
        out_specs=(
            P(("node", "local", "replica"), None),
            P("replica", ("node", "local"), None, None),
            P(("node", "local"), "replica", None),
        ),
        check_vma=False,
    )
```

profile of v0, /device:TPU:1, one launch (start us, length us, event | category | flops | bytes accessed | tf_op | source)
XLA Modules:
  0.0 338.8 jit_solution(17193811881308216589)
XLA Ops:
  7.2 0.8 broadcast_subtract_fusion
  8.2 0.8 copy.42
  10.6 0.7 add_select_fusion.1
  11.3 1.4 fusion.2
  12.7 4.0 %convolution_convert_fusion = bf16[768,3584]{1,0:T(8,128)(2,1)} fusion(pred[768,128]{1,0:T(8,128)(4,1)S(1)} %fusion.2, bf16[128,3584]{1,0:T(8,128)(2,1)S(1)} %copy-done), kind=kOutput, calls=%fused_computation.4 | convolution fusion | flops 707395584 | bytes 6520832 | tf_op jit(solution)/shard_map/dot_general | solution.py:36
  16.7 9.6 %reshape.174 = bf16[128,6,3584]{2,1,0:T(8,128)(2,1)} reshape(bf16[768,3584]{1,0:T(8,128)(2,1)} %convolution_convert_fusion) | data formatting | bytes 11010048 | tf_op jit(solution)/shard_map/reshape | solution.py:42
  26.3 16.8 %all-to-all-start = ((bf16[128,6,3584]{2,1,0:T(8,128)(2,1)}), bf16[128,6,3584]{2,1,0:T(8,128)(2,1)}, u32[]{:S(2)}, u32[]{:S(2)}) async-start(bf16[128,6,3584]{2,1,0:T(8,128)(2,1)} %reshape.174), calls=%async_computation | async-start | bytes 14680064 | tf_op jit(solution)/shard_map/all_to_all | solution.py:41
  43.1 0.7 all-gather.3.cloned.1.call-update
  44.3 162.7 %all-to-all-done = bf16[128,6,3584]{2,1,0:T(8,128)(2,1)} async-done(((bf16[128,6,3584]{2,1,0:T(8,128)(2,1)}), bf16[128,6,3584]{2,1,0:T(8,128)(2,1)}, u32[]{:S(2)}, u32[]{:S(2)}) %all-to-all-start) | async-done | bytes 5505056 | tf_op jit(solution)/shard_map/all_to_all | solution.py:41
  207.0 9.7 %reshape.175 = bf16[768,3584]{1,0:T(8,128)(2,1)} reshape(bf16[128,6,3584]{2,1,0:T(8,128)(2,1)} %all-to-all-done) | data formatting | bytes 11010048 | tf_op jit(solution)/shard_map/reshape | solution.py:56
  216.6 10.9 %multiply_reduce_fusion = (f32[768]{0:T(1024)S(1)}, f32[768,1024]{1,0:T(8,128)}) fusion(bf16[1,1,768,1024]{3,2,1,0:T(8,128)(2,1)S(1)} %copy-done.3, bf16[768,3584]{1,0:T(8,128)(2,1)} %reshape.175, bf16[1,3584,1024]{2,1,0:T(8,128)(2,1)} %all-gather.3.cloned.1.call-done), kind=kOutput, calls=%fused_computation.9 | convolution fusion | flops 5639502848 | bytes 17566720 | tf_op jit(solution)/shard_map/dot_general | solution.py:61
  227.6 0.8 all_to_all.14
  228.3 6.1 %all-to-all-start.1 = ((f32[128,1,6]{2,1,0:T(1,128)}), f32[128,1,6]{2,1,0:T(1,128)S(1)}, u32[]{:S(2)}, u32[]{:S(2)}) async-start(f32[128,1,6]{2,1,0:T(1,128)} %bitcast.5), calls=%async_computation.1 | async-start | bytes 131072 | tf_op jit(solution)/shard_map/all_to_all | solution.py:79
  234.5 10.4 %all-to-all-done.1 = f32[128,1,6]{2,1,0:T(1,128)S(1)} async-done(((f32[128,1,6]{2,1,0:T(1,128)}), f32[128,1,6]{2,1,0:T(1,128)S(1)}, u32[]{:S(2)}, u32[]{:S(2)}) %all-to-all-start.1) | async-done | bytes 3104 | tf_op jit(solution)/shard_map/all_to_all | solution.py:79
  245.5 0.8 reduce.7
  246.4 4.5 %gather_fusion = f32[1024]{0:T(1024)S(1)} fusion(f32[768]{0:T(1024)S(1)} %reshape.177, s32[1024]{0:T(1024)S(1)} %broadcast_clamp_fusion), kind=kCustom, calls=%fused_computation | custom fusion | bytes 12288 | tf_op jit(solution)/shard_map/gather | solution.py:88
  251.2 0.6 fusion.12
  252.5 16.3 %all_to_all.20 = bf16[128,1,6]{2,1,0:T(2,128)(2,1)S(1)} all-to-all(bf16[128,1,6]{2,1,0:T(2,128)(2,1)S(1)} %convert_element_type.86), channel_id=1, replica_groups=mesh['node'=16,'local'=8,'replica'=2] {'node','local'}, dimensions={0} | all-to-all | bytes 3072 | tf_op jit(solution)/shard_map/all_to_all | solution.py:48
  268.9 8.2 %multiply_convert_fusion = bf16[128,6,3584]{2,1,0:T(8,128)(2,1)} fusion(bf16[128,6,3584]{2,1,0:T(8,128)(2,1)} %all-to-all-done, f32[128,6]{1,0:T(8,128)S(1)} %bitcast.27), kind=kLoop, calls=%fused_computation.1 | loop fusion | flops 8257536 | bytes 11013120 | tf_op jit(solution)/shard_map/convert_element_type | solution.py:68
  277.1 9.7 %convert_element_type.81 = bf16[768,3584]{1,0:T(8,128)(2,1)} reshape(bf16[128,6,3584]{2,1,0:T(8,128)(2,1)} %multiply_convert_fusion) | data formatting | bytes 11010048 | tf_op jit(solution)/shard_map/convert_element_type | solution.py:68
  286.8 11.7 %fusion.4 = f32[3584,1024]{1,0:T(8,128)} fusion(bf16[768,3584]{1,0:T(8,128)(2,1)} %convert_element_type.81, bf16[1,1,768,1024]{3,2,1,0:T(8,128)(2,1)S(1)} %copy-done.3), kind=kOutput, calls=%fused_computation.13 | convolution fusion | flops 5637144576 | bytes 21757952 | tf_op jit(solution)/shard_map/dot_general | solution.py:71
  298.8 3.3 fusion.3
  302.2 24.3 %reduce-scatter.2.cloned.1.call-done = f32[1792,1024]{1,0:T(8,128)} async-done(((f32[3584,1024]{1,0:T(8,128)}), f32[1792,1024]{1,0:T(8,128)}) %reduce-scatter.2.cloned.1.call-update) | async-done | bytes 7340048 | tf_op jit(solution)/shard_map/reduce_scatter | solution.py:70
  326.5 5.5 %convert_bitcast_fusion = bf16[1,1792,1024]{2,1,0:T(8,128)(2,1)} fusion(f32[1792,1024]{1,0:T(8,128)} %reduce-scatter.2.cloned.1.call-done), kind=kLoop, calls=%fused_computation.5 | loop fusion | flops 1835008 | bytes 11010048 | tf_op jit(solution)/shard_map/reshape | solution.py:78
  (48 shorter events, 4.4 us)
Async XLA Ops:
  7.2 5.6 %copy-start = (bf16[128,3584]{1,0:T(8,128)(2,1)S(1)}, bf16[128,3584]{1,0:T(8,128)(2,1)}, u32[]{:S(2)}) copy-start(bf16[128,3584]{1,0:T(8,128)(2,1)} %param.6) | copy-start | bytes 2752516
  26.3 180.7 %all-to-all-start = ((bf16[128,6,3584]{2,1,0:T(8,128)(2,1)}), bf16[128,6,3584]{2,1,0:T(8,128)(2,1)}, u32[]{:S(2)}, u32[]{:S(2)}) async-start(bf16[128,6,3584]{2,1,0:T(8,128)(2,1)} %reshape.174), calls=%async_computation | async-start | bytes 14680064 | tf_op jit(solution)/shard_map/all_to_all | solution.py:41
  43.1 173.5 %all-gather.3.cloned.1.call-start = ((), (), s32[]{:S(2)}) async-start(), calls=%async_computation.5 | async-start | bytes 11010048 | tf_op jit(solution)/shard_map/all_gather | solution.py:63
  44.3 172.3 %copy-start.3 = (bf16[1,1,768,1024]{3,2,1,0:T(8,128)(2,1)S(1)}, bf16[1,1,768,1024]{3,2,1,0:T(8,128)(2,1)}, u32[]{:S(2)}) copy-start(bf16[1,1,768,1024]{3,2,1,0:T(8,128)(2,1)} %param.10) | copy-start | bytes 4718596
  216.6 34.5 %copy-start.2 = (f32[128,8]{0,1:T(8,128)S(1)}, f32[128,8]{0,1:T(8,128)}, u32[]{:S(2)}) copy-start(f32[128,8]{0,1:T(8,128)} %param.9) | copy-start | bytes 12292
  228.3 16.6 %all-to-all-start.1 = ((f32[128,1,6]{2,1,0:T(1,128)}), f32[128,1,6]{2,1,0:T(1,128)S(1)}, u32[]{:S(2)}, u32[]{:S(2)}) async-start(f32[128,1,6]{2,1,0:T(1,128)} %bitcast.5), calls=%async_computation.1 | async-start | bytes 131072 | tf_op jit(solution)/shard_map/all_to_all | solution.py:79
  234.5 92.0 %reduce-scatter.2.cloned.1.call-start = ((), (), s32[]{:S(2)}) async-start(), calls=%async_computation.4 | async-start | bytes 22020096 | tf_op jit(solution)/shard_map/reduce_scatter | solution.py:70
  298.8 33.1 %copy-start.1 = (bf16[128,3584]{1,0:T(8,128)(2,1)S(1)}, bf16[128,3584]{1,0:T(8,128)(2,1)}, u32[]{:S(2)}) copy-start(bf16[128,3584]{1,0:T(8,128)(2,1)} %param.6) | copy-start | bytes 2752516
Sparse Core Ops, SparseCore 0:
  45.7 25.5 all-gather.2
  298.6 27.8 reduce-scatter.1
where the time goes:
time: 340 us; the launch traced here: 339 us
  waiting for transfers between devices  198 us (58%)
  local copies, waits for them, and re-layouts  37.6 us (11%)
  matrix products  26.6 us (8%)
  other arithmetic  23 us (7%)
  starting transfers between devices  23 us (7%)
  blocking collectives  16.3 us (5%)
  between operations  14.2 us (4%)
    all_to_all x1, waiting for transfers between devices, local(): lax.all_to_all(send_rows.reshape(experts, capacity, width), ('node', 'loc...  163 us
    reduce_scatter x1, waiting for transfers between devices, local(): lax.psum_scatter(lax.dot_general(columns, hidden, (((0,), (0,)), ((), ())...  24.3 us
    all_to_all x1, starting transfers between devices, local(): lax.all_to_all(send_rows.reshape(experts, capacity, width), ('node', 'loc...  16.8 us
    all_to_all x1, blocking collectives, local(): lax.all_to_all(send_gate.reshape(experts, capacity), ('node', 'local'), s...  16.3 us
    dot_general x1, matrix products, local(): lax.dot_general(columns, hidden, (((0,), (0,)), ((), ())), preferred_elem...  11.7 us
    dot_general x1, matrix products, local(): jnp.dot(columns, lax.all_gather(weight_local, 'replica', axis=0, tiled=Tr...  10.9 us
    all_to_all x1, waiting for transfers between devices, local(): lax.all_to_all(gate_grad.reshape(experts, capacity), ('node', 'local'), s...  10.4 us
    convert_element_type x1, local copies, waits for them, and re-layouts, local(): (slot_gate[:, None] * got_rows.astype(jnp.float32)).astype(jnp.bfloat16)  9.68 us
  transfers between devices with their start and end apart: 4, of which 3 were waited for; matrix products, arithmetic and copies ran while one was open for 4% of the time, Pallas kernels for 0%

commit v1 on v0

v1 whole, which is shorter than its diff:
```python
import functools

import jax
import jax.numpy as jnp
from jax import lax
from jax.experimental import pallas as pl
from jax.experimental.pallas import tpu as pltpu
from jax.sharding import PartitionSpec as P

route_scale = 2.5
bf16 = jnp.bfloat16
f32 = jnp.float32
EARLY = 1280
NODES = 16
RING = 8
CAP = 6
TOPK = 8
BLOCK = RING * CAP
LANES = 128
SLOTS = NODES * BLOCK
RING_SPLIT = 1152
VMEM_LIMIT = 14 * 2**20


def route_kernel(z_ref, *refs):
    infos, (select_ref, gate_ref) = refs[:RING], refs[RING:]
    slots = SLOTS
    z = z_ref[0]
    expert = (lax.broadcasted_iota(jnp.int32, (NODES, LANES), 0) * RING + z).astype(f32)
    before = (
        lax.broadcasted_iota(jnp.int32, (LANES, LANES), 0)
        < lax.broadcasted_iota(jnp.int32, (LANES, LANES), 1)
    ).astype(bf16)
    spread = (
        lax.broadcasted_iota(jnp.int32, (slots, NODES), 0) // BLOCK
        == lax.broadcasted_iota(jnp.int32, (slots, NODES), 1)
    ).astype(bf16)
    row = lax.broadcasted_iota(jnp.int32, (slots, LANES), 0) % BLOCK
    source = row // CAP
    wanted = (row % CAP + 1).astype(f32)
    slot_gate = jnp.zeros((slots, LANES), f32)
    for j in range(RING):
        info = infos[j][...].astype(f32).T
        code, gate = info[:TOPK], info[TOPK : 2 * TOPK]
        match = jnp.zeros((NODES, LANES), f32)
        match_gate = jnp.zeros((NODES, LANES), f32)
        for k in range(TOPK):
            hit = expert == code[k : k + 1]
            match = match + jnp.where(hit, 1.0, 0.0)
            match_gate = match_gate + jnp.where(hit, gate[k : k + 1], 0.0)
        rank = jnp.dot(match.astype(bf16), before, preferred_element_type=f32)
        order = (match * (rank + 1.0)).astype(bf16)
        order = jnp.dot(spread, order, preferred_element_type=f32)
        spread_gate = jnp.dot(spread, match_gate.astype(bf16), preferred_element_type=f32)
        origin = lax.rem(z + RING - j, RING)
        here = (order == wanted) & (source == origin)
        block = jnp.where(here, 1.0, 0.0).astype(bf16)
        select_ref[:, j * LANES : (j + 1) * LANES] = block
        slot_gate = slot_gate + jnp.where(here, spread_gate, 0.0)
    total = jnp.sum(slot_gate, axis=1, keepdims=True)
    gate_ref[...] = jnp.broadcast_to(total, (slots, LANES)).astype(bf16)


def route(z, pieces, column):
    whole = pl.BlockSpec((SLOTS, RING * LANES), lambda i: (0, 0))
    codes = [
        pl.BlockSpec((LANES, LANES), lambda i, at=column if piece.shape[1] > LANES else 0: (0, at // LANES))
        for piece in pieces
    ]
    return pl.pallas_call(
        route_kernel,
        grid=(1,),
        out_shape=(
            jax.ShapeDtypeStruct((SLOTS, RING * LANES), bf16),
            jax.ShapeDtypeStruct((SLOTS, LANES), bf16),
        ),
        in_specs=[pl.BlockSpec(memory_space=pltpu.SMEM)] + codes,
        out_specs=(whole, pl.BlockSpec((SLOTS, LANES), lambda i: (0, 0))),
        compiler_params=pltpu.CompilerParams(vmem_limit_bytes=VMEM_LIMIT),
        cost_estimate=pl.CostEstimate(flops=10**8, bytes_accessed=2 * 10**6, transcendentals=0),
        name="route",
    )(z, *pieces)


def pack_kernel(halfway, select_ref, gate_ref, *refs):
    pieces, (first_ref, second_ref), out_ref = refs[: RING - 1], refs[RING - 1 : RING + 1], refs[-1]
    middle = RING // 2
    step = pl.program_id(0)

    @pl.when(step < 2 * halfway)
    def _():
        far = jnp.where(step < halfway, first_ref[...], second_ref[...])
        rows = [piece[...] for piece in pieces]
        rows = jnp.concatenate(rows[:middle] + [far] + rows[middle:], axis=0)
        out_ref[...] = jnp.dot(select_ref[...], rows, preferred_element_type=f32).astype(bf16)

    @pl.when(step == 2 * halfway)
    def _():
        out_ref[:, :LANES] = gate_ref[...]


def pack(select, gate_column, pieces, first, second):
    tile = 384
    halfway = RING_SPLIT // tile
    width = 2 * RING_SPLIT
    near = pl.BlockSpec((LANES, tile), lambda i: (0, jnp.minimum(i, 2 * halfway - 1)))
    middle = RING // 2
    return pl.pallas_call(
        functools.partial(pack_kernel, halfway),
        grid=(2 * halfway + 1,),
        out_shape=jax.ShapeDtypeStruct((SLOTS, width + LANES), bf16),
        in_specs=[
            pl.BlockSpec((SLOTS, RING * LANES), lambda i: (0, 0)),
            pl.BlockSpec((SLOTS, LANES), lambda i: (0, 0)),
        ]
        + [near] * (RING - 1)
        + [
            pl.BlockSpec((LANES, tile), lambda i: (0, jnp.minimum(i, halfway - 1))),
            pl.BlockSpec((LANES, tile), lambda i: (0, jnp.clip(i - halfway, 0, halfway - 1))),
        ],
        out_specs=pl.BlockSpec((SLOTS, tile), lambda i: (0, i)),
        compiler_params=pltpu.CompilerParams(vmem_limit_bytes=VMEM_LIMIT),
        cost_estimate=pl.CostEstimate(
            flops=2 * SLOTS * RING * LANES * width,
            bytes_accessed=2 * width * (SLOTS + RING * LANES) + 2 * SLOTS * RING * LANES,
            transcendentals=0,
        ),
        name="pack",
    )(select, gate_column, *pieces[:middle], *pieces[middle + 1 :], first, second)


def ranks(code):
    expert = lax.broadcasted_iota(jnp.int32, (LANES, LANES), 0).astype(f32)
    match = jnp.zeros((LANES, LANES), f32)
    for k in range(TOPK):
        match = match + jnp.where(expert == code[k : k + 1], 1.0, 0.0)
    before = (
        lax.broadcasted_iota(jnp.int32, (LANES, LANES), 0)
        < lax.broadcasted_iota(jnp.int32, (LANES, LANES), 1)
    ).astype(bf16)
    return expert, match, jnp.dot(match.astype(bf16), before, preferred_element_type=f32)


def choose(code):
    unused, match, rank = ranks(code)
    order = (match * (rank + 1.0)).astype(bf16)
    row = lax.broadcasted_iota(jnp.int32, (SLOTS, LANES), 0)
    spread = (row // CAP == lax.broadcasted_iota(jnp.int32, (SLOTS, LANES), 1)).astype(bf16)
    order = jnp.dot(spread, order, preferred_element_type=f32)
    return order == (row % CAP + 1).astype(f32)


def own_kernel(info_ref, x_ref, *refs):
    out_ref, chosen_ref = refs[-2:]

    @pl.when(pl.program_id(0) == 0)
    def _():
        chosen = choose(info_ref[...].astype(f32).T[:TOPK])
        chosen_ref[...] = jnp.where(chosen, 1.0, 0.0).astype(bf16)

    out_ref[...] = jnp.dot(chosen_ref[...], x_ref[...], preferred_element_type=f32).astype(bf16)


def own_slots(info, x, later):
    width = x.shape[1]
    tile = 256
    return pl.pallas_call(
        own_kernel,
        grid=(width // tile,),
        out_shape=jax.ShapeDtypeStruct((SLOTS, width), bf16),
        in_specs=[
            pl.BlockSpec((LANES, LANES), lambda i: (0, 0)),
            pl.BlockSpec((LANES, tile), lambda i: (0, i)),
        ]
        + [pl.BlockSpec(memory_space=pl.ANY)] * len(later),
        out_specs=pl.BlockSpec((SLOTS, tile), lambda i: (0, i)),
        scratch_shapes=[pltpu.VMEM((SLOTS, LANES), bf16)],
        compiler_params=pltpu.CompilerParams(vmem_limit_bytes=VMEM_LIMIT),
        cost_estimate=pl.CostEstimate(
            flops=2 * SLOTS * LANES * width, bytes_accessed=2 * SLOTS * width, transcendentals=0
        ),
        name="own_slots",
    )(info, x, *later)


def moved_rows(z, turned):
    place = lax.broadcasted_iota(jnp.int32, (SLOTS, SLOTS), 0 if turned else 1)
    moved = lax.broadcasted_iota(jnp.int32, (SLOTS, SLOTS), 1 if turned else 0)
    step, rest = moved // (NODES * CAP), moved % (NODES * CAP)
    at = lax.rem(z + (RING - step if turned else step), RING)
    return jnp.where(place == rest // CAP * BLOCK + at * CAP + rest % CAP, 1.0, 0.0).astype(bf16)


def turn_kernel(z_ref, x_ref, *refs):
    outs, move_ref = refs[:-1], refs[-1]

    @pl.when(pl.program_id(0) == 0)
    def _():
        move_ref[...] = moved_rows(z_ref[0], False)

    rows = jnp.dot(move_ref[...], x_ref[...], preferred_element_type=f32).astype(bf16)
    part, middle = NODES * CAP, RING // 2
    blocks = [rows[k * part : (k + 1) * part] for k in range(RING)]
    blocks[2] = jnp.concatenate([blocks[2], blocks[middle][: part // 2]], axis=0)
    blocks[-2] = jnp.concatenate([blocks[-2], blocks[middle][part // 2 :]], axis=0)
    for out, block in zip(outs, blocks[:middle] + blocks[middle + 1 :]):
        out[...] = block


def turn(z, x):
    width = x.shape[1]
    tile = 256
    part = NODES * CAP
    heights = [part, part, part + part // 2, part, part, part + part // 2, part]
    return pl.pallas_call(
        turn_kernel,
        grid=(width // tile,),
        out_shape=[jax.ShapeDtypeStruct((height, width), bf16) for height in heights],
        in_specs=[
            pl.BlockSpec(memory_space=pltpu.SMEM),
            pl.BlockSpec((SLOTS, tile), lambda i: (0, i)),
        ],
        out_specs=[pl.BlockSpec((height, tile), lambda i: (0, i)) for height in heights],
        scratch_shapes=[pltpu.VMEM((SLOTS, SLOTS), bf16)],
        compiler_params=pltpu.CompilerParams(vmem_limit_bytes=VMEM_LIMIT),
        cost_estimate=pl.CostEstimate(
            flops=2 * SLOTS * SLOTS * width, bytes_accessed=4 * SLOTS * width, transcendentals=0
        ),
        name="turn",
    )(z, x)


def cross(blocks):
    def step(x, k):
        return lax.ppermute(x, "local", [(i, (i + k) % RING) for i in range(RING)])

    part = NODES * CAP
    zero, one, two, three, back3, back2, back1 = blocks
    two, back2 = step(two, 2), step(back2, -2)
    ahead, behind = step(two[part:], 2), step(back2[part:], -2)
    return [zero, step(one, 1), two, step(three, 3), ahead, behind, step(back3, -3), back2, step(back1, -1)]


def settle_kernel(z_ref, *refs):
    pieces, out_ref, move_ref = refs[:-2], refs[-2], refs[-1]

    @pl.when(pl.program_id(0) == 0)
    def _():
        move_ref[...] = moved_rows(z_ref[0], True)

    rows = jnp.concatenate([piece[...] for piece in pieces], axis=0)
    out_ref[...] = jnp.dot(move_ref[...], rows, preferred_element_type=f32).astype(bf16)


def settle(z, pieces):
    width = pieces[0].shape[1]
    tile = 256
    return pl.pallas_call(
        settle_kernel,
        grid=(width // tile,),
        out_shape=jax.ShapeDtypeStruct((SLOTS, width), bf16),
        in_specs=[pl.BlockSpec(memory_space=pltpu.SMEM)]
        + [
            pl.BlockSpec((min(piece.shape[0], NODES * CAP), tile), lambda i: (0, i))
            for piece in pieces
        ],
        out_specs=pl.BlockSpec((SLOTS, tile), lambda i: (0, i)),
        scratch_shapes=[pltpu.VMEM((SLOTS, SLOTS), bf16)],
        compiler_params=pltpu.CompilerParams(vmem_limit_bytes=VMEM_LIMIT),
        cost_estimate=pl.CostEstimate(
            flops=2 * SLOTS * SLOTS * width, bytes_accessed=4 * SLOTS * width, transcendentals=0
        ),
        name="settle",
    )(z, *pieces)


def halves_kernel(up_ref, down_ref, *refs):
    refs[-2][...] = up_ref[...]
    refs[-1][...] = down_ref[...]


def halves(up, down, later):
    tile = 384
    steps = RING_SPLIT // tile
    line = lambda i: (0, i)
    return pl.pallas_call(
        halves_kernel,
        grid=(steps,),
        out_shape=(jax.ShapeDtypeStruct((LANES, RING_SPLIT), bf16),) * 2,
        in_specs=[
            pl.BlockSpec((LANES, tile), line),
            pl.BlockSpec((LANES, tile), lambda i: (0, i + steps)),
        ]
        + [pl.BlockSpec(memory_space=pl.ANY)] * len(later),
        out_specs=(pl.BlockSpec((LANES, tile), line),) * 2,
        compiler_params=pltpu.CompilerParams(vmem_limit_bytes=VMEM_LIMIT),
        cost_estimate=pl.CostEstimate(flops=0, bytes_accessed=10**6, transcendentals=0),
        name="halves",
    )(up, down, *later)


def ring(block):
    ahead = [(i, (i + 1) % RING) for i in range(RING)]
    back = [(i, (i - 1) % RING) for i in range(RING)]
    pieces = [block] + [None] * (RING - 1)
    up = down = block
    for step in range(1, RING // 2):
        up = lax.ppermute(up, "local", ahead)
        down = lax.ppermute(down, "local", back)
        pieces[step], pieces[RING - step] = up, down
    return pieces


def farthest(up, down, later):
    ahead = [(i, (i + 1) % RING) for i in range(RING)]
    back = [(i, (i - 1) % RING) for i in range(RING)]
    first, second = halves(up, down, later)
    return lax.ppermute(first, "local", ahead), lax.ppermute(second, "local", back)


def back_kernel(half, rows_ref, acc_ref, hidden_ref, other_ref, own_ref, grad_ref, sums_ref, gated_ref):
    wide = half + own_ref.shape[0]
    total = acc_ref[...]
    total = total + jnp.dot(rows_ref[:, :half], other_ref[...], preferred_element_type=f32)
    total = total + jnp.dot(rows_ref[:, half:wide], own_ref[...], preferred_element_type=f32)
    gate = rows_ref[:, wide : wide + 1].astype(f32)
    hidden = hidden_ref[...].astype(f32)
    grad_ref[...] = (gate * total).astype(bf16)
    gated_ref[...] = (gate * hidden).astype(bf16)
    sums_ref[...] = jnp.sum(hidden * total, axis=1, keepdims=True)


def back(rows, acc, hidden, weight_other, weight_own, rest):
    tile = 192
    half, units = weight_other.shape
    line = lambda i: (i, 0)
    still = lambda i: (0, 0)
    return pl.pallas_call(
        functools.partial(back_kernel, half),
        grid=(SLOTS // tile,),
        out_shape=(
            jax.ShapeDtypeStruct((SLOTS, units), bf16),
            jax.ShapeDtypeStruct((SLOTS, 1), f32),
            jax.ShapeDtypeStruct((SLOTS, units), bf16),
        ),
        in_specs=[
            pl.BlockSpec((tile, rows.shape[1]), line),
            pl.BlockSpec((tile, units), line),
            pl.BlockSpec((tile, units), line),
            pl.BlockSpec((half, units), still),
            pl.BlockSpec((rest, units), still),
        ],
        out_specs=(
            pl.BlockSpec((tile, units), line),
            pl.BlockSpec((tile, 1), line),
            pl.BlockSpec((tile, units), line),
        ),
        compiler_params=pltpu.CompilerParams(vmem_limit_bytes=24 * 2**20),
        cost_estimate=pl.CostEstimate(
            flops=2 * SLOTS * units * (half + rest), bytes_accessed=16 * 10**6, transcendentals=0
        ),
        name="back",
    )(rows, acc, hidden, weight_other, weight_own)


def down_kernel(steps, x_ref, y_ref, gated_ref, received_ref, out_ref):
    step = pl.program_id(0)
    rows = jnp.where(step < steps, x_ref[...], y_ref[...])
    share = lax.dot_general(rows, gated_ref[...], (((0,), (0,)), ((), ())), preferred_element_type=f32)
    out_ref[...] = (share + received_ref[...].astype(f32)).astype(bf16)


def down(x, skip, y, gated, received):
    tile = 256
    steps = (x.shape[1] - skip) // tile
    more = y.shape[1] // tile
    units = gated.shape[1]
    return pl.pallas_call(
        functools.partial(down_kernel, steps),
        grid=(steps + more,),
        out_shape=jax.ShapeDtypeStruct(received.shape, bf16),
        in_specs=[
            pl.BlockSpec((SLOTS, tile), lambda i: (0, skip // tile + jnp.minimum(i, steps - 1))),
            pl.BlockSpec((SLOTS, tile), lambda i: (0, jnp.maximum(i - steps, 0))),
            pl.BlockSpec((SLOTS, units), lambda i: (0, 0)),
            pl.BlockSpec((tile, units), lambda i: (i, 0)),
        ],
        out_specs=pl.BlockSpec((tile, units), lambda i: (i, 0)),
        compiler_params=pltpu.CompilerParams(vmem_limit_bytes=VMEM_LIMIT),
        cost_estimate=pl.CostEstimate(
            flops=2 * SLOTS * units * received.shape[0], bytes_accessed=12 * 10**6, transcendentals=0
        ),
        name="down",
    )(x, y, gated, received)


def finish_kernel(info_ref, logits_ref, value_ref, *refs):
    out_ref = refs[-1]
    code = info_ref[...].astype(f32).T[:TOPK]
    expert, match, rank = ranks(code)
    value = jnp.zeros((LANES, LANES), f32)
    for c in range(CAP):
        value = jnp.where(rank == float(c), value_ref[:, c : c + 1], value)
    value = jnp.where(match > 0.0, value, 0.0)
    pairs = [
        jnp.sum(jnp.where(expert == code[k : k + 1], value, 0.0), axis=0, keepdims=True)
        for k in range(TOPK)
    ]
    pair_grad = jnp.concatenate(pairs, axis=0)
    affinity = 1.0 / (1.0 + jnp.exp(-logits_ref[...]))
    denominator = jnp.sum(affinity, axis=0, keepdims=True)
    weighted = jnp.sum(pair_grad * affinity, axis=0, keepdims=True)
    grad = route_scale * (pair_grad / denominator - weighted / (denominator * denominator))
    out_ref[...] = grad * affinity * (1.0 - affinity)


def finish(info, logits, value, later):
    vmem = pl.BlockSpec(memory_space=pltpu.VMEM)
    return pl.pallas_call(
        finish_kernel,
        out_shape=jax.ShapeDtypeStruct(logits.shape, f32),
        in_specs=[vmem] * 3 + [pl.BlockSpec(memory_space=pl.ANY)] * len(later),
        out_specs=vmem,
        compiler_params=pltpu.CompilerParams(vmem_limit_bytes=VMEM_LIMIT),
        cost_estimate=pl.CostEstimate(flops=10**7, bytes_accessed=10**6, transcendentals=10**4),
        name="finish",
    )(info, logits, value, *later)


def local(out_grad, expert_ids, drop_flags, router_logits, saved_hidden, down_weight):
    slot_total = saved_hidden.shape[2]
    tok_rows = out_grad.shape[0]
    top_count = expert_ids.shape[1]
    half = out_grad.shape[1] // 2
    experts = NODES * RING
    z = lax.axis_index("local")
    copy = lax.axis_index("replica")
    swap = [(0, 1), (1, 0)]

    affinity = jax.nn.sigmoid(router_logits)
    denominator = jnp.sum(affinity, axis=1, keepdims=True)
    gate_sent = (route_scale * affinity / denominator).astype(bf16)
    code = jnp.where(drop_flags == 0, expert_ids, -1).astype(bf16)
    info = jnp.concatenate([code, gate_sent], axis=1)
    info = jnp.pad(info, ((0, 0), (0, LANES - 2 * top_count)))

    weight_own = down_weight.reshape(half, down_weight.shape[2])
    weight_other = lax.ppermute(weight_own, "replica", swap)
    hidden = saved_hidden.reshape(slot_total, saved_hidden.shape[3])

    low, high = out_grad[:, :half], out_grad[:, half:]
    other, own = jnp.where(copy == 0, high, low), jnp.where(copy == 0, low, high)
    at = z.reshape(1)
    rest = half - EARLY
    wide = half + rest

    middle = RING // 2
    pieces = ring(jnp.concatenate([other, own[:, :rest], info], axis=1))
    far_info = lax.ppermute(info, "local", [(i, (i + middle) % RING) for i in range(RING)])

    early = own_slots(info, own[:, rest:], ())
    early = early.reshape(NODES, BLOCK, EARLY)
    early = lax.all_to_all(early, "node", split_axis=0, concat_axis=0, tiled=True)
    early = turn(at, early.reshape(slot_total, EARLY))
    first, second = farthest(pieces[middle - 1], pieces[middle + 1], (early[0],))
    crossed = cross(early)
    select, gate_column = route(at, pieces[:middle] + [far_info] + pieces[middle + 1 :], wide)
    rows = pack(select, gate_column, pieces, first, second)
    rows = rows.reshape(NODES, BLOCK, wide + LANES)
    rows = lax.all_to_all(rows, "node", split_axis=0, concat_axis=0, tiled=True)
    rows = rows.reshape(slot_total, wide + LANES)

    early = settle(at, crossed)
    acc = jnp.dot(early, weight_own[rest:], preferred_element_type=f32)
    grad_hidden, gate_grad, gated = back(rows, acc, hidden, weight_other, weight_own, rest)
    grad_hidden = grad_hidden.reshape(saved_hidden.shape)
    returned = lax.all_to_all(
        gate_grad.reshape(experts, CAP),
        ("node", "local"),
        split_axis=0,
        concat_axis=0,
        tiled=True,
    )
    received = lax.dot_general(
        rows[:, :half], gated, (((0,), (0,)), ((), ())), preferred_element_type=f32
    )
    received = lax.ppermute(received.astype(bf16), "replica", swap)
    grad_down = down(rows[:, half:wide], 0, early, gated, received)
    grad_logits = finish(info, router_logits.T, returned, (grad_down,)).T
    return (grad_logits, grad_hidden, grad_down.reshape(down_weight.shape))


def solution(mesh):
    return jax.shard_map(
        local,
        mesh=mesh,
        in_specs=(
            P(("node", "local", "replica"), None),
            P(("node", "local", "replica"), None),
            P(("node", "local", "replica"), None),
            P(("node", "local", "replica"), None),
            P("replica", ("node", "local"), None, None),
            P(("node", "local"), "replica", None),
        ),
        out_specs=(
            P(("node", "local", "replica"), None),
            P("replica", ("node", "local"), None, None),
            P(("node", "local"), "replica", None),
        ),
        check_vma=False,
    )
```

time: 340 us -> 201 us (0.59)
  waiting for transfers between devices: 198 us -> 60.4 us
  starting transfers between devices: 23 us -> 71 us
  Pallas kernels: 0 us -> 41.9 us
  local copies, waits for them, and re-layouts: 37.6 us -> 9.54 us
  other arithmetic: 23 us -> 4.57 us
  blocking collectives: 16.3 us -> 0 us
  matrix products: 26.6 us -> 11.7 us
  between operations: 14.2 us -> 0.98 us
    all_to_all x2 -> x3, waiting for transfers between devices: 173 us -> 1.03 us  [the longest x1 1.03 us: local(): lax.all_to_all(gate_grad.reshape(experts, CAP), ('node', 'local'), split_...]
    ppermute x0 -> x19, waiting for transfers between devices: none -> 59.4 us  [the longest x3 32 us: ring(): up = lax.ppermute(up, 'local', ahead)]
    ppermute x0 -> x19, starting transfers between devices: none -> 45.4 us  [the longest x8 16.5 us: step(): return lax.ppermute(x, 'local', [(i, (i + k) % RING) for i in range(RING)])]
    pallas_call x0 -> x9, Pallas kernels: none -> 41.9 us  [the longest x1 9.05 us: pack(): pl.pallas_call(functools.partial(pack_kernel, halfway), grid=(2 * halfway...]
    reduce_scatter x1 -> x0, waiting for transfers between devices: 24.3 us -> none  [local(): lax.psum_scatter(lax.dot_general(columns, hidden, (((0,), (0,)), ((), ())...]
    reshape x3 -> x0, local copies, waits for them, and re-layouts: 19.4 us -> none  [the longest x1 9.66 us: local(): got_rows = got_rows.reshape(slot_total, width)]
    all_to_all x1 -> x0, blocking collectives: 16.3 us -> none  [local(): lax.all_to_all(send_gate.reshape(experts, capacity), ('node', 'local'), s...]
    dot_general x3 -> x2, matrix products: 26.6 us -> 11.7 us  [the longest x1 7 us: local(): lax.dot_general(rows[:, :half], gated, (((0,), (0,)), ((), ())), preferre...]
  transfers between devices with their start and end apart: 4 -> 22, of which waited for: 3 -> 9; matrix products, arithmetic and copies ran while one was open for 4% -> 4% of each run, Pallas kernels for 0% -> 14%
where the time goes in v1:
time: 201 us; the launch traced here: 200 us
  starting transfers between devices  71 us (35%)
  waiting for transfers between devices  60.4 us (30%)
  Pallas kernels  41.9 us (21%)
  matrix products  11.7 us (6%)
  local copies, waits for them, and re-layouts  9.54 us (5%)
  other arithmetic  4.57 us (2%)
    ppermute x3, waiting for transfers between devices, ring(): up = lax.ppermute(up, 'local', ahead)  32 us
    ppermute x8, waiting for transfers between devices, step(): return lax.ppermute(x, 'local', [(i, (i + k) % RING) for i in range(RING)])  27.4 us
    ppermute x8, starting transfers between devices, step(): return lax.ppermute(x, 'local', [(i, (i + k) % RING) for i in range(RING)])  16.5 us
    all_to_all x1, starting transfers between devices, local(): lax.all_to_all(gate_grad.reshape(experts, CAP), ('node', 'local'), split_...  12 us
    ppermute x3, starting transfers between devices, ring(): down = lax.ppermute(down, 'local', back)  9.37 us
    pallas_call x1, Pallas kernels, pack(): pl.pallas_call(functools.partial(pack_kernel, halfway), grid=(2 * halfway...  9.05 us
    pallas_call x1, Pallas kernels, back(): pl.pallas_call(functools.partial(back_kernel, half), grid=(SLOTS // tile,...  8.37 us
    pallas_call x1, Pallas kernels, down(): pl.pallas_call(functools.partial(down_kernel, steps), grid=(steps + more,...  8.09 us
  transfers between devices with their start and end apart: 22, of which 9 were waited for; matrix products, arithmetic and copies ran while one was open for 4% of the time, Pallas kernels for 14%

profile of v1, /device:TPU:1, one launch (start us, length us, event | category | flops | bytes accessed | tf_op | source)
XLA Modules:
  0.0 200.1 jit_solution(13643963419459461443)
XLA Ops:
  4.2 3.5 %own_slots.1 = bf16[768,1280]{1,0:T(8,128)(2,1)} custom-call(bf16[128,128]{1,0:T(8,128)(2,1)S(1)} %pad.4.info_ref, bf16[128,1280]{1,0:T(8,128)(2,1)S(1)} %slice.41.x_ref), custom_call_target="tpu_custom_call" | custom-call | flops 251658240 | bytes 1966080 | tf_op jit(solution)/shard_map/own_slots/pallas_call | solution.py:167
  7.6 7.6 %all-to-all-start = ((bf16[16,48,1280]{2,1,0:T(8,128)(2,1)}), bf16[16,48,1280]{2,1,0:T(8,128)(2,1)}, u32[]{:S(2)}, u32[]{:S(2)}) async-start(bf16[16,48,1280]{2,1,0:T(8,128)(2,1)} %bitcast.2), calls=%async_computation | async-start | bytes 3932160 | tf_op jit(solution)/shard_map/all_to_all | solution.py:463
  17.1 4.0 %collective-permute-start.4 = (bf16[128,2432]{1,0:T(8,128)(2,1)S(1)}, bf16[128,2432]{1,0:T(8,128)(2,1)S(1)}, u32[]{:S(2)}, u32[]{:S(2)}) collective-permute-start(bf16[128,2432]{1,0:T(8,128)(2,1)S(1)} %pad_maximum_fusion.refs_0_), channel_id=1, source_target_pairs={{0,14},{2,0},{4,2},{6,4},{8,6},{10,8},{12,10},{14,12},{1,15},{3,1}... | collective-permute-start | bytes 1867784 | tf_op jit(solution)/shard_map/ppermute | solution.py:309
  21.1 13.4 %collective-permute-done.refs_1_ = bf16[128,2432]{1,0:T(8,128)(2,1)S(1)} collective-permute-done((bf16[128,2432]{1,0:T(8,128)(2,1)S(1)}, bf16[128,2432]{1,0:T(8,128)(2,1)S(1)}, u32[]{:S(2)}, u32[]{:S(2)}) %collective-permute-start) | collective-permute-done | bytes 622624 | tf_op jit(solution)/shard_map/ppermute | solution.py:308
  37.2 12.7 %collective-permute-done.1.refs_2_ = bf16[128,2432]{1,0:T(8,128)(2,1)} collective-permute-done((bf16[128,2432]{1,0:T(8,128)(2,1)S(1)}, bf16[128,2432]{1,0:T(8,128)(2,1)}, u32[]{:S(2)}, u32[]{:S(2)}) %collective-permute-start.1) | collective-permute-done | bytes 622624 | tf_op jit(solution)/shard_map/ppermute | solution.py:308
  52.6 5.3 %turn.1 = (bf16[96,1280]{1,0:T(8,128)(2,1)S(1)}, bf16[96,1280]{1,0:T(8,128)(2,1)S(1)}, bf16[144,1280]{1,0:T(8,128)(2,1)S(1)}, bf16[96,1280]{1,0:T(8,128)(2,1)S(1...) custom-call(s32[1]{0:T(128)} %bitcast.1.z_ref, ...), custom_call_target="tpu_custom_call" | custom-call | flops 1509949440 | bytes 3932160 | tf_op jit(solution)/shard_map/turn/pallas_call | solution.py:215
  58.7 5.8 %collective-permute-done.2.refs_3_.up_ref = bf16[128,2432]{1,0:T(8,128)(2,1)S(1)} collective-permute-done((bf16[128,2432]{1,0:T(8,128)(2,1)}, bf16[128,2432]{1,0:T(8,128)(2,1)S(1)}, u32[]{:S(2)}, u32[]{:S(2)}) %collective-permute-start.2) | collective-permute-done | bytes 622624 | tf_op jit(solution)/shard_map/ppermute | solution.py:308
  67.7 3.0 %collective-permute-start.3 = (bf16[128,128]{1,0:T(8,128)(2,1)S(1)}, bf16[128,128]{1,0:T(8,128)(2,1)S(1)}, u32[]{:S(2)}, u32[]{:S(2)}) collective-permute-start(bf16[128,128]{1,0:T(8,128)(2,1)S(1)} %pad.4.info_ref), channel_id=1, source_target_pairs={{0,8},{2,10},{4,12},{6,14},{8,0},{10,2},{12,4},{14,6},{1,9},{3,11}... | collective-permute-start | bytes 98312 | tf_op jit(solution)/shard_map/ppermute | solution.py:459
  70.7 4.5 %collective-permute-start.17 = (bf16[1792,1024]{1,0:T(8,128)(2,1)}, bf16[1792,1024]{1,0:T(8,128)(2,1)}, u32[]{:S(2)}, u32[]{:S(2)}) collective-permute-start(bf16[1792,1024]{1,0:T(8,128)(2,1)} %bitcast.8.own_ref), channel_id=1, source_target_pairs={{0,1},{1,0},{2,3},{3,2},{4,5},{5,4},{6,7},{7,6},{8,9},{9,8},{10,11... | collective-permute-start | bytes 11010056 | tf_op jit(solution)/shard_map/ppermute | solution.py:448
  75.2 3.3 %route.1 = (bf16[768,1024]{1,0:T(8,128)(2,1)S(1)}, bf16[768,128]{1,0:T(8,128)(2,1)S(1)}) custom-call(s32[1]{0:T(128)} %bitcast.1.z_ref, bf16[128,2432]{1,0:T(8,128)(2,1)S(1)} %pad_maximum_fusion.refs_0_, bf16[128,2432]{1,0:T(8,128)(2,1)S(1)} %collective-permute-done.refs_1_, bf16[128,2432]{1,0:T(8,128)(2,1)} %collective-permute-done.1.refs_2_, ...), custom_call_target="tpu_custom_call" | custom-call | flops 100000000 | bytes 2000000 | tf_op jit(solution)/shard_map/route/pallas_call | solution.py:70
  78.5 9.0 %pack.1 = bf16[768,2432]{1,0:T(8,128)(2,1)S(1)} custom-call(bf16[768,1024]{1,0:T(8,128)(2,1)S(1)} %get-tuple-element.17.select_ref, bf16[768,128]{1,0:T(8,128)(2,1)S(1)} %get-tuple-element.18.gate_ref, bf16[128,2432]{1,0:T(8,128)(2,1)S(1)} %pad_maximum_fusion.refs_0_, bf16[128,2432]{1,0:T(8,128)(2,1)S(1)} %collective-permute-done.refs_1_, ...), custom_call_target="tpu_custom_call" | custom-call | flops 3623878656 | bytes 9830400 | tf_op jit(solution)/shard_map/pack/pallas_call | solution.py:108
  89.4 6.0 %all-to-all-start.1 = ((bf16[16,48,2432]{2,1,0:T(8,128)(2,1)}), bf16[16,48,2432]{2,1,0:T(8,128)(2,1)}, u32[]{:S(2)}, u32[]{:S(2)}) async-start(bf16[16,48,2432]{2,1,0:T(8,128)(2,1)} %bitcast.19), calls=%async_computation.1 | async-start | bytes 7471104 | tf_op jit(solution)/shard_map/all_to_all | solution.py:470
  95.6 3.6 %collective-permute-start.13 = (bf16[144,1280]{1,0:T(8,128)(2,1)S(1)}, bf16[144,1280]{1,0:T(8,128)(2,1)S(1)}, u32[]{:S(2)}, u32[]{:S(2)}) collective-permute-start(bf16[144,1280]{1,0:T(8,128)(2,1)S(1)} %copy-done.10), channel_id=1, source_target_pairs={{0,12},{2,14},{4,0},{6,2},{8,4},{10,6},{12,8},{14,10},{1,13},{3,15... | collective-permute-start | bytes 1105928 | tf_op jit(solution)/shard_map/ppermute | solution.py:235
  102.1 9.5 %collective-permute-done.10.refs_2_ = bf16[144,1280]{1,0:T(8,128)(2,1)S(1)} collective-permute-done((bf16[144,1280]{1,0:T(8,128)(2,1)S(1)}, bf16[144,1280]{1,0:T(8,128)(2,1)S(1)}, u32[]{:S(2)}, u32[]{:S(2)}) %collective-permute-start.10) | collective-permute-done | bytes 368672 | tf_op jit(solution)/shard_map/ppermute | solution.py:235
  115.8 4.2 %collective-permute-start.12 = (bf16[48,1280]{1,0:T(8,128)(2,1)S(1)}, bf16[48,1280]{1,0:T(8,128)(2,1)S(1)}, u32[]{:S(2)}, u32[]{:S(2)}) collective-permute-start(bf16[48,1280]{1,0:T(8,128)(2,1)S(1)} %slice.42), channel_id=1, source_target_pairs={{0,4},{2,6},{4,8},{6,10},{8,12},{10,14},{12,0},{14,2},{1,5},{3,7},... | collective-permute-start | bytes 368648 | tf_op jit(solution)/shard_map/ppermute | solution.py:235
  120.1 7.9 %collective-permute-done.11.refs_3_ = bf16[96,1280]{1,0:T(8,128)(2,1)S(1)} collective-permute-done((bf16[96,1280]{1,0:T(8,128)(2,1)S(1)}, bf16[96,1280]{1,0:T(8,128)(2,1)S(1)}, u32[]{:S(2)}, u32[]{:S(2)}) %collective-permute-start.11) | collective-permute-done | bytes 245792 | tf_op jit(solution)/shard_map/ppermute | solution.py:235
  128.0 3.4 %collective-permute-start.14 = (bf16[48,1280]{1,0:T(8,128)(2,1)S(1)}, bf16[48,1280]{1,0:T(8,128)(2,1)S(1)}, u32[]{:S(2)}, u32[]{:S(2)}) collective-permute-start(bf16[48,1280]{1,0:T(8,128)(2,1)S(1)} %slice.43), channel_id=1, source_target_pairs={{0,12},{2,14},{4,0},{6,2},{8,4},{10,6},{12,8},{14,10},{1,13},{3,15... | collective-permute-start | bytes 368648 | tf_op jit(solution)/shard_map/ppermute | solution.py:235
  131.4 8.1 %collective-permute-done.12.refs_4_ = bf16[48,1280]{1,0:T(8,128)(2,1)S(1)} collective-permute-done((bf16[48,1280]{1,0:T(8,128)(2,1)S(1)}, bf16[48,1280]{1,0:T(8,128)(2,1)S(1)}, u32[]{:S(2)}, u32[]{:S(2)}) %collective-permute-start.12) | collective-permute-done | bytes 122912 | tf_op jit(solution)/shard_map/ppermute | solution.py:235
  142.5 4.7 %fusion.1.acc_ref = f32[768,1024]{1,0:T(8,128)S(1)} fusion(bf16[768,1280]{1,0:T(8,128)(2,1)S(1)} %settle.1.y_ref, bf16[1,1792,1024]{2,1,0:T(8,128)(2,1)} %param.11), kind=kOutput, calls=%fused_computation.2 | convolution fusion | flops 2013265920 | bytes 7733248 | tf_op jit(solution)/shard_map/dot_general | solution.py:474
  148.6 8.4 %back.1 = (bf16[768,1024]{1,0:T(8,128)(2,1)}, f32[768,1]{1,0:T(8,128)S(1)}, bf16[768,1024]{1,0:T(8,128)(2,1)S(1)}) custom-call(bf16[768,2432]{1,0:T(8,128)(2,1)} %bitcast.5.rows_ref, f32[768,1024]{1,0:T(8,128)S(1)} %fusion.1.acc_ref, bf16[768,1024]{1,0:T(8,128)(2,1)S(1)} %bitcast.20, bf16[1792,1024]{1,0:T(8,128)(2,1)} %collective-permute-done.17.other_ref, ...), custom_call_target="tpu_custom_call" | custom-call | flops 3623878656 | bytes 16000000 | tf_op jit(solution)/shard_map/back/pallas_call | solution.py:338
  157.0 7.0 %convolution_convert_fusion = bf16[1792,1024]{1,0:T(8,128)(2,1)} fusion(bf16[768,1024]{1,0:T(8,128)(2,1)S(1)} %get-tuple-element.29.gated_ref, bf16[768,2432]{1,0:T(8,128)(2,1)} %bitcast.5.rows_ref), kind=kOutput, calls=%fused_computation | convolution fusion | flops 2820407296 | bytes 7995392 | tf_op jit(solution)/shard_map/dot_general | solution.py:484
  164.0 7.5 %collective-permute-start.18 = (bf16[1792,1024]{1,0:T(8,128)(2,1)}, bf16[1792,1024]{1,0:T(8,128)(2,1)}, u32[]{:S(2)}, u32[]{:S(2)}) collective-permute-start(bf16[1792,1024]{1,0:T(8,128)(2,1)} %convolution_convert_fusion), channel_id=1, source_target_pairs={{0,1},{1,0},{2,3},{3,2},{4,5},{5,4},{6,7},{7,6},{8,9},{9,8},{10,11... | collective-permute-start | bytes 11010056 | tf_op jit(solution)/shard_map/ppermute | solution.py:487
  174.7 12.0 %all-to-all-start.2 = ((f32[128,1,6]{2,1,0:T(1,128)}), f32[128,1,6]{2,1,0:T(1,128)S(1)}, u32[]{:S(2)}, u32[]{:S(2)}) async-start(f32[128,1,6]{2,1,0:T(1,128)} %bitcast.9), calls=%async_computation.2 | async-start | bytes 131072 | tf_op jit(solution)/shard_map/all_to_all | solution.py:477
  188.1 8.1 %down.1.refs_0_ = bf16[1792,1024]{1,0:T(8,128)(2,1)} custom-call(bf16[768,512]{1,0:T(8,128)(2,1)S(1)} %slice.44.x_ref, bf16[768,1280]{1,0:T(8,128)(2,1)S(1)} %copy-done.3, bf16[768,1024]{1,0:T(8,128)(2,1)S(1)} %copy-done.5, bf16[1792,1024]{1,0:T(8,128)(2,1)} %collective-permute-done.18.received_ref), custom_call_target="tpu_custom_call" | custom-call | flops 2818572288 | bytes 12000000 | tf_op jit(solution)/shard_map/down/pallas_call | solution.py:378
  (88 shorter events, 36.7 us)
Async XLA Ops:
  7.6 45.0 %all-to-all-start = ((bf16[16,48,1280]{2,1,0:T(8,128)(2,1)}), bf16[16,48,1280]{2,1,0:T(8,128)(2,1)}, u32[]{:S(2)}, u32[]{:S(2)}) async-start(bf16[16,48,1280]{2,1,0:T(8,128)(2,1)} %bitcast.2), calls=%async_computation | async-start | bytes 3932160 | tf_op jit(solution)/shard_map/all_to_all | solution.py:463
  15.3 19.2 %collective-permute-start = (bf16[128,2432]{1,0:T(8,128)(2,1)S(1)}, bf16[128,2432]{1,0:T(8,128)(2,1)S(1)}, u32[]{:S(2)}, u32[]{:S(2)}) collective-permute-start(bf16[128,2432]{1,0:T(8,128)(2,1)S(1)} %pad_maximum_fusion.refs_0_), channel_id=1, source_target_pairs={{0,2},{2,4},{4,6},{6,8},{8,10},{10,12},{12,14},{14,0},{1,3},{3,5},... | collective-permute-start | bytes 1867784 | tf_op jit(solution)/shard_map/ppermute | solution.py:308
  17.1 17.5 %collective-permute-start.4 = (bf16[128,2432]{1,0:T(8,128)(2,1)S(1)}, bf16[128,2432]{1,0:T(8,128)(2,1)S(1)}, u32[]{:S(2)}, u32[]{:S(2)}) collective-permute-start(bf16[128,2432]{1,0:T(8,128)(2,1)S(1)} %pad_maximum_fusion.refs_0_), channel_id=1, source_target_pairs={{0,14},{2,0},{4,2},{6,4},{8,6},{10,8},{12,10},{14,12},{1,15},{3,1}... | collective-permute-start | bytes 1867784 | tf_op jit(solution)/shard_map/ppermute | solution.py:309
  34.5 15.4 %collective-permute-start.1 = (bf16[128,2432]{1,0:T(8,128)(2,1)S(1)}, bf16[128,2432]{1,0:T(8,128)(2,1)}, u32[]{:S(2)}, u32[]{:S(2)}) collective-permute-start(bf16[128,2432]{1,0:T(8,128)(2,1)S(1)} %collective-permute-done.refs_1_), channel_id=1, source_target_pairs={{0,2},{2,4},{4,6},{6,8},{8,10},{10,12},{12,14},{14,0},{1,3},{3,5},... | collective-permute-start | bytes 1867784 | tf_op jit(solution)/shard_map/ppermute | solution.py:308
  34.5 15.4 %collective-permute-start.5 = (bf16[128,2432]{1,0:T(8,128)(2,1)S(1)}, bf16[128,2432]{1,0:T(8,128)(2,1)}, u32[]{:S(2)}, u32[]{:S(2)}) collective-permute-start(bf16[128,2432]{1,0:T(8,128)(2,1)S(1)} %collective-permute-done.4.refs_7_.refs_6_), channel_id=1, source_target_pairs={{0,14},{2,0},{4,2},{6,4},{8,6},{10,8},{12,10},{14,12},{1,15},{3,1}... | collective-permute-start | bytes 1867784 | tf_op jit(solution)/shard_map/ppermute | solution.py:309
  49.9 14.6 %collective-permute-start.2 = (bf16[128,2432]{1,0:T(8,128)(2,1)}, bf16[128,2432]{1,0:T(8,128)(2,1)S(1)}, u32[]{:S(2)}, u32[]{:S(2)}) collective-permute-start(bf16[128,2432]{1,0:T(8,128)(2,1)} %collective-permute-done.1.refs_2_), channel_id=1, source_target_pairs={{0,2},{2,4},{4,6},{6,8},{8,10},{10,12},{12,14},{14,0},{1,3},{3,5},... | collective-permute-start | bytes 1867784 | tf_op jit(solution)/shard_map/ppermute | solution.py:308
  49.9 14.6 %collective-permute-start.6 = (bf16[128,2432]{1,0:T(8,128)(2,1)}, bf16[128,2432]{1,0:T(8,128)(2,1)S(1)}, u32[]{:S(2)}, u32[]{:S(2)}) collective-permute-start(bf16[128,2432]{1,0:T(8,128)(2,1)} %collective-permute-done.5.refs_6_.refs_5_), channel_id=1, source_target_pairs={{0,14},{2,0},{4,2},{6,4},{8,6},{10,8},{12,10},{14,12},{1,15},{3,1}... | collective-permute-start | bytes 1867784 | tf_op jit(solution)/shard_map/ppermute | solution.py:309
  64.9 13.6 %collective-permute-start.7 = (bf16[128,1152]{1,0:T(8,128)(2,1)S(1)}, bf16[128,1152]{1,0:T(8,128)(2,1)S(1)}, u32[]{:S(2)}, u32[]{:S(2)}) collective-permute-start(bf16[128,1152]{1,0:T(8,128)(2,1)S(1)} %get-tuple-element.20), channel_id=1, source_target_pairs={{0,2},{2,4},{4,6},{6,8},{8,10},{10,12},{12,14},{14,0},{1,3},{3,5},... | collective-permute-start | bytes 884744 | tf_op jit(solution)/shard_map/ppermute | solution.py:318
  65.0 13.5 %collective-permute-start.8 = (bf16[128,1152]{1,0:T(8,128)(2,1)S(1)}, bf16[128,1152]{1,0:T(8,128)(2,1)S(1)}, u32[]{:S(2)}, u32[]{:S(2)}) collective-permute-start(bf16[128,1152]{1,0:T(8,128)(2,1)S(1)} %get-tuple-element.21), channel_id=1, source_target_pairs={{0,14},{2,0},{4,2},{6,4},{8,6},{10,8},{12,10},{14,12},{1,15},{3,1}... | collective-permute-start | bytes 884744 | tf_op jit(solution)/shard_map/ppermute | solution.py:318
  67.7 7.5 %collective-permute-start.3 = (bf16[128,128]{1,0:T(8,128)(2,1)S(1)}, bf16[128,128]{1,0:T(8,128)(2,1)S(1)}, u32[]{:S(2)}, u32[]{:S(2)}) collective-permute-start(bf16[128,128]{1,0:T(8,128)(2,1)S(1)} %pad.4.info_ref), channel_id=1, source_target_pairs={{0,8},{2,10},{4,12},{6,14},{8,0},{10,2},{12,4},{14,6},{1,9},{3,11}... | collective-permute-start | bytes 98312 | tf_op jit(solution)/shard_map/ppermute | solution.py:459
  70.7 76.5 %collective-permute-start.17 = (bf16[1792,1024]{1,0:T(8,128)(2,1)}, bf16[1792,1024]{1,0:T(8,128)(2,1)}, u32[]{:S(2)}, u32[]{:S(2)}) collective-permute-start(bf16[1792,1024]{1,0:T(8,128)(2,1)} %bitcast.8.own_ref), channel_id=1, source_target_pairs={{0,1},{1,0},{2,3},{3,2},{4,5},{5,4},{6,7},{7,6},{8,9},{9,8},{10,11... | collective-permute-start | bytes 11010056 | tf_op jit(solution)/shard_map/ppermute | solution.py:448
  89.4 22.2 %copy-start.14 = (bf16[96,1280]{1,0:T(8,128)(2,1)S(1)}, bf16[96,1280]{1,0:T(8,128)(2,1)}, u32[]{:S(2)}) copy-start(bf16[96,1280]{1,0:T(8,128)(2,1)} %copy-done.13) | copy-start | bytes 737284
  89.4 57.8 %all-to-all-start.1 = ((bf16[16,48,2432]{2,1,0:T(8,128)(2,1)}), bf16[16,48,2432]{2,1,0:T(8,128)(2,1)}, u32[]{:S(2)}, u32[]{:S(2)}) async-start(bf16[16,48,2432]{2,1,0:T(8,128)(2,1)} %bitcast.19), calls=%async_computation.1 | async-start | bytes 7471104 | tf_op jit(solution)/shard_map/all_to_all | solution.py:470
  95.5 16.1 %collective-permute-start.10 = (bf16[144,1280]{1,0:T(8,128)(2,1)S(1)}, bf16[144,1280]{1,0:T(8,128)(2,1)S(1)}, u32[]{:S(2)}, u32[]{:S(2)}) collective-permute-start(bf16[144,1280]{1,0:T(8,128)(2,1)S(1)} %copy-done.12), channel_id=1, source_target_pairs={{0,4},{2,6},{4,8},{6,10},{8,12},{10,14},{12,0},{14,2},{1,5},{3,7},... | collective-permute-start | bytes 1105928 | tf_op jit(solution)/shard_map/ppermute | solution.py:235
  95.6 16.0 %collective-permute-start.13 = (bf16[144,1280]{1,0:T(8,128)(2,1)S(1)}, bf16[144,1280]{1,0:T(8,128)(2,1)S(1)}, u32[]{:S(2)}, u32[]{:S(2)}) collective-permute-start(bf16[144,1280]{1,0:T(8,128)(2,1)S(1)} %copy-done.10), channel_id=1, source_target_pairs={{0,12},{2,14},{4,0},{6,2},{8,4},{10,6},{12,8},{14,10},{1,13},{3,15... | collective-permute-start | bytes 1105928 | tf_op jit(solution)/shard_map/ppermute | solution.py:235
  99.1 16.7 %collective-permute-start.9 = (bf16[96,1280]{1,0:T(8,128)(2,1)S(1)}, bf16[96,1280]{1,0:T(8,128)(2,1)S(1)}, u32[]{:S(2)}, u32[]{:S(2)}) collective-permute-start(bf16[96,1280]{1,0:T(8,128)(2,1)S(1)} %copy-done.20), channel_id=1, source_target_pairs={{0,2},{2,4},{4,6},{6,8},{8,10},{10,12},{12,14},{14,0},{1,3},{3,5},... | collective-permute-start | bytes 737288 | tf_op jit(solution)/shard_map/ppermute | solution.py:235
  99.1 28.8 %collective-permute-start.11 = (bf16[96,1280]{1,0:T(8,128)(2,1)S(1)}, bf16[96,1280]{1,0:T(8,128)(2,1)S(1)}, u32[]{:S(2)}, u32[]{:S(2)}) collective-permute-start(bf16[96,1280]{1,0:T(8,128)(2,1)S(1)} %copy-done.18), channel_id=1, source_target_pairs={{0,6},{2,8},{4,10},{6,12},{8,14},{10,0},{12,2},{14,4},{1,7},{3,9},... | collective-permute-start | bytes 737288 | tf_op jit(solution)/shard_map/ppermute | solution.py:235
  111.6 19.8 %collective-permute-start.15 = (bf16[96,1280]{1,0:T(8,128)(2,1)S(1)}, bf16[96,1280]{1,0:T(8,128)(2,1)S(1)}, u32[]{:S(2)}, u32[]{:S(2)}) collective-permute-start(bf16[96,1280]{1,0:T(8,128)(2,1)S(1)} %copy-done.16), channel_id=1, source_target_pairs={{0,10},{2,12},{4,14},{6,0},{8,2},{10,4},{12,6},{14,8},{1,11},{3,13... | collective-permute-start | bytes 737288 | tf_op jit(solution)/shard_map/ppermute | solution.py:235
  111.6 19.8 %collective-permute-start.16 = (bf16[96,1280]{1,0:T(8,128)(2,1)S(1)}, bf16[96,1280]{1,0:T(8,128)(2,1)S(1)}, u32[]{:S(2)}, u32[]{:S(2)}) collective-permute-start(bf16[96,1280]{1,0:T(8,128)(2,1)S(1)} %copy-done.14), channel_id=1, source_target_pairs={{0,14},{2,0},{4,2},{6,4},{8,6},{10,8},{12,10},{14,12},{1,15},{3,1}... | collective-permute-start | bytes 737288 | tf_op jit(solution)/shard_map/ppermute | solution.py:235
  115.8 23.7 %collective-permute-start.12 = (bf16[48,1280]{1,0:T(8,128)(2,1)S(1)}, bf16[48,1280]{1,0:T(8,128)(2,1)S(1)}, u32[]{:S(2)}, u32[]{:S(2)}) collective-permute-start(bf16[48,1280]{1,0:T(8,128)(2,1)S(1)} %slice.42), channel_id=1, source_target_pairs={{0,4},{2,6},{4,8},{6,10},{8,12},{10,14},{12,0},{14,2},{1,5},{3,7},... | collective-permute-start | bytes 368648 | tf_op jit(solution)/shard_map/ppermute | solution.py:235
  128.0 11.5 %collective-permute-start.14 = (bf16[48,1280]{1,0:T(8,128)(2,1)S(1)}, bf16[48,1280]{1,0:T(8,128)(2,1)S(1)}, u32[]{:S(2)}, u32[]{:S(2)}) collective-permute-start(bf16[48,1280]{1,0:T(8,128)(2,1)S(1)} %slice.43), channel_id=1, source_target_pairs={{0,12},{2,14},{4,0},{6,2},{8,4},{10,6},{12,8},{14,10},{1,13},{3,15... | collective-permute-start | bytes 368648 | tf_op jit(solution)/shard_map/ppermute | solution.py:235
  164.0 22.6 %copy-start.3 = (bf16[768,1280]{1,0:T(8,128)(2,1)S(1)}, bf16[768,1280]{1,0:T(8,128)(2,1)}, u32[]{:S(2)}) copy-start(bf16[768,1280]{1,0:T(8,128)(2,1)} %copy-done.2) | copy-start | bytes 5898244
  164.0 22.6 %collective-permute-start.18 = (bf16[1792,1024]{1,0:T(8,128)(2,1)}, bf16[1792,1024]{1,0:T(8,128)(2,1)}, u32[]{:S(2)}, u32[]{:S(2)}) collective-permute-start(bf16[1792,1024]{1,0:T(8,128)(2,1)} %convolution_convert_fusion), channel_id=1, source_target_pairs={{0,1},{1,0},{2,3},{3,2},{4,5},{5,4},{6,7},{7,6},{8,9},{9,8},{10,11... | collective-permute-start | bytes 11010056 | tf_op jit(solution)/shard_map/ppermute | solution.py:487
  174.7 22.5 %all-to-all-start.2 = ((f32[128,1,6]{2,1,0:T(1,128)}), f32[128,1,6]{2,1,0:T(1,128)S(1)}, u32[]{:S(2)}, u32[]{:S(2)}) async-start(f32[128,1,6]{2,1,0:T(1,128)} %bitcast.9), calls=%async_computation.2 | async-start | bytes 131072 | tf_op jit(solution)/shard_map/all_to_all | solution.py:477
  (19 other events, 178.3 us)

commit v2 on v1

--- a/solution.py
+++ b/solution.py
@@ -20,6 +20,27 @@
 SLOTS = NODES * BLOCK
 RING_SPLIT = 1152
 VMEM_LIMIT = 14 * 2**20
+
+
+def codes_kernel(ids_ref, drop_ref, logits_ref, out_ref):
+    code = jnp.where(drop_ref[...] == 0, ids_ref[...], -1).astype(f32)
+    affinity = 1.0 / (1.0 + jnp.exp(-logits_ref[...]))
+    gate = route_scale * affinity / jnp.sum(affinity, axis=0, keepdims=True)
+    rest = jnp.zeros((LANES - 2 * TOPK, LANES), f32)
+    out_ref[...] = jnp.concatenate([code, gate, rest], axis=0).T.astype(bf16)
+
+
+def codes(expert_ids, drop_flags, router_logits):
+    vmem = pl.BlockSpec(memory_space=pltpu.VMEM)
+    return pl.pallas_call(
+        codes_kernel,
+        out_shape=jax.ShapeDtypeStruct((LANES, LANES), bf16),
+        in_specs=[vmem] * 3,
+        out_specs=vmem,
+        compiler_params=pltpu.CompilerParams(vmem_limit_bytes=VMEM_LIMIT),
+        cost_estimate=pl.CostEstimate(flops=10**5, bytes_accessed=10**5, transcendentals=10**3),
+        name="codes",
+    )(expert_ids.T, drop_flags.T, router_logits.T)
 
 
 def route_kernel(z_ref, *refs):
@@ -63,7 +84,7 @@
 
 def route(z, pieces, column):
     whole = pl.BlockSpec((SLOTS, RING * LANES), lambda i: (0, 0))
-    codes = [
+    blocks = [
         pl.BlockSpec((LANES, LANES), lambda i, at=column if piece.shape[1] > LANES else 0: (0, at // LANES))
         for piece in pieces
     ]
@@ -74,7 +95,7 @@
             jax.ShapeDtypeStruct((SLOTS, RING * LANES), bf16),
             jax.ShapeDtypeStruct((SLOTS, LANES), bf16),
         ),
-        in_specs=[pl.BlockSpec(memory_space=pltpu.SMEM)] + codes,
+        in_specs=[pl.BlockSpec(memory_space=pltpu.SMEM)] + blocks,
         out_specs=(whole, pl.BlockSpec((SLOTS, LANES), lambda i: (0, 0))),
         compiler_params=pltpu.CompilerParams(vmem_limit_bytes=VMEM_LIMIT),
         cost_estimate=pl.CostEstimate(flops=10**8, bytes_accessed=2 * 10**6, transcendentals=0),
@@ -108,7 +129,7 @@
     return pl.pallas_call(
         functools.partial(pack_kernel, halfway),
         grid=(2 * halfway + 1,),
-        out_shape=jax.ShapeDtypeStruct((SLOTS, width + LANES), bf16),
+        out_shape=pltpu.HBM((SLOTS, width + LANES), bf16),
         in_specs=[
             pl.BlockSpec((SLOTS, RING * LANES), lambda i: (0, 0)),
             pl.BlockSpec((SLOTS, LANES), lambda i: (0, 0)),
@@ -318,52 +339,65 @@
     return lax.ppermute(first, "local", ahead), lax.ppermute(second, "local", back)
 
 
-def back_kernel(half, rows_ref, acc_ref, hidden_ref, other_ref, own_ref, grad_ref, sums_ref, gated_ref):
-    wide = half + own_ref.shape[0]
-    total = acc_ref[...]
-    total = total + jnp.dot(rows_ref[:, :half], other_ref[...], preferred_element_type=f32)
-    total = total + jnp.dot(rows_ref[:, half:wide], own_ref[...], preferred_element_type=f32)
+def back_kernel(rest, rows_ref, early_ref, hidden_ref, other_ref, own_ref, grad_ref, sums_ref, gated_ref):
+    half = other_ref.shape[0]
+    wide = half + rest
+    total = jnp.dot(rows_ref[:, :half], other_ref[...], preferred_element_type=f32)
+    total = total + jnp.dot(rows_ref[:, half:wide], own_ref[:rest], preferred_element_type=f32)
+    total = total + jnp.dot(early_ref[...], own_ref[rest:], preferred_element_type=f32)
     gate = rows_ref[:, wide : wide + 1].astype(f32)
     hidden = hidden_ref[...].astype(f32)
     grad_ref[...] = (gate * total).astype(bf16)
     gated_ref[...] = (gate * hidden).astype(bf16)
-    sums_ref[...] = jnp.sum(hidden * total, axis=1, keepdims=True)
-
-
-def back(rows, acc, hidden, weight_other, weight_own, rest):
-    tile = 192
+    tile = rows_ref.shape[0]
+    sums = jnp.sum(hidden * total, axis=1, keepdims=True)
+    lane = lax.broadcasted_iota(jnp.int32, (tile, LANES), 1)
+    rank = lax.broadcasted_iota(jnp.int32, (tile, LANES), 0) % CAP
+    expert = lax.broadcasted_iota(jnp.int32, (tile // CAP, tile), 0)
+    gather = jnp.where(expert == lax.broadcasted_iota(jnp.int32, expert.shape, 1) // CAP, 1.0, 0.0)
+    sums_ref[...] = jnp.dot(
+        gather,
+        jnp.where(lane == rank, sums, 0.0),
+        precision=lax.Precision.HIGHEST,
+        preferred_element_type=f32,
+    )
+
+
+def back(rows, early, hidden, weight_other, weight_own):
+    tile = 384
     half, units = weight_other.shape
     line = lambda i: (i, 0)
-    still = lambda i: (0, 0)
-    return pl.pallas_call(
-        functools.partial(back_kernel, half),
+    still = pl.BlockSpec((half, units), lambda i: (0, 0), pipeline_mode=pl.Buffered(1))
+    return pl.pallas_call(
+        functools.partial(back_kernel, half - early.shape[1]),
         grid=(SLOTS // tile,),
         out_shape=(
             jax.ShapeDtypeStruct((SLOTS, units), bf16),
-            jax.ShapeDtypeStruct((SLOTS, 1), f32),
+            jax.ShapeDtypeStruct((SLOTS // CAP, LANES), f32),
             jax.ShapeDtypeStruct((SLOTS, units), bf16),
         ),
         in_specs=[
             pl.BlockSpec((tile, rows.shape[1]), line),
+            pl.BlockSpec((tile, early.shape[1]), line),
             pl.BlockSpec((tile, units), line),
-            pl.BlockSpec((tile, units), line),
-            pl.BlockSpec((half, units), still),
-            pl.BlockSpec((rest, units), still),
+            still,
+            still,
         ],
         out_specs=(
             pl.BlockSpec((tile, units), line),
-            pl.BlockSpec((tile, 1), line),
+            pl.BlockSpec((tile // CAP, LANES), line),
             pl.BlockSpec((tile, units), line),
         ),
-        compiler_params=pltpu.CompilerParams(vmem_limit_bytes=24 * 2**20),
+        compiler_params=pltpu.CompilerParams(vmem_limit_bytes=32 * 2**20),
         cost_estimate=pl.CostEstimate(
-            flops=2 * SLOTS * units * (half + rest), bytes_accessed=16 * 10**6, transcendentals=0
+            flops=4 * SLOTS * units * half, bytes_accessed=18 * 10**6, transcendentals=0
         ),
         name="back",
-    )(rows, acc, hidden, weight_other, weight_own)
-
-
-def down_kernel(steps, x_ref, y_ref, gated_ref, received_ref, out_ref):
+    )(rows, early, hidden, weight_other, weight_own)
+
+
+def down_kernel(steps, x_ref, y_ref, gated_ref, received_ref, out_ref, mark_ref):
+    mark_ref[...] = jnp.zeros_like(mark_ref)
     step = pl.program_id(0)
     rows = jnp.where(step < steps, x_ref[...], y_ref[...])
     share = lax.dot_general(rows, gated_ref[...], (((0,), (0,)), ((), ())), preferred_element_type=f32)
@@ -372,20 +406,26 @@
 
 def down(x, skip, y, gated, received):
     tile = 256
-    steps = (x.shape[1] - skip) // tile
     more = y.shape[1] // tile
+    steps = received.shape[0] // tile - more
     units = gated.shape[1]
     return pl.pallas_call(
         functools.partial(down_kernel, steps),
         grid=(steps + more,),
-        out_shape=jax.ShapeDtypeStruct(received.shape, bf16),
+        out_shape=(
+            jax.ShapeDtypeStruct(received.shape, bf16),
+            jax.ShapeDtypeStruct((8, LANES), f32),
+        ),
         in_specs=[
             pl.BlockSpec((SLOTS, tile), lambda i: (0, skip // tile + jnp.minimum(i, steps - 1))),
             pl.BlockSpec((SLOTS, tile), lambda i: (0, jnp.maximum(i - steps, 0))),
             pl.BlockSpec((SLOTS, units), lambda i: (0, 0)),
             pl.BlockSpec((tile, units), lambda i: (i, 0)),
         ],
-        out_specs=pl.BlockSpec((tile, units), lambda i: (i, 0)),
+        out_specs=(
+            pl.BlockSpec((tile, units), lambda i: (i, 0)),
+            pl.BlockSpec((8, LANES), lambda i: (0, 0)),
+        ),
         compiler_params=pltpu.CompilerParams(vmem_limit_bytes=VMEM_LIMIT),
         cost_estimate=pl.CostEstimate(
             flops=2 * SLOTS * units * received.shape[0], bytes_accessed=12 * 10**6, transcendentals=0
@@ -429,20 +469,13 @@
 
 def local(out_grad, expert_ids, drop_flags, router_logits, saved_hidden, down_weight):
     slot_total = saved_hidden.shape[2]
-    tok_rows = out_grad.shape[0]
-    top_count = expert_ids.shape[1]
     half = out_grad.shape[1] // 2
     experts = NODES * RING
     z = lax.axis_index("local")
     copy = lax.axis_index("replica")
     swap = [(0, 1), (1, 0)]
 
-    affinity = jax.nn.sigmoid(router_logits)
-    denominator = jnp.sum(affinity, axis=1, keepdims=True)
-    gate_sent = (route_scale * affinity / denominator).astype(bf16)
-    code = jnp.where(drop_flags == 0, expert_ids, -1).astype(bf16)
-    info = jnp.concatenate([code, gate_sent], axis=1)
-    info = jnp.pad(info, ((0, 0), (0, LANES - 2 * top_count)))
+    info = codes(expert_ids, drop_flags, router_logits)
 
     weight_own = down_weight.reshape(half, down_weight.shape[2])
     weight_other = lax.ppermute(weight_own, "replica", swap)
@@ -462,7 +495,7 @@
     early = early.reshape(NODES, BLOCK, EARLY)
     early = lax.all_to_all(early, "node", split_axis=0, concat_axis=0, tiled=True)
     early = turn(at, early.reshape(slot_total, EARLY))
-    first, second = farthest(pieces[middle - 1], pieces[middle + 1], (early[0],))
+    first, second = farthest(pieces[middle - 1], pieces[middle + 1], ())
     crossed = cross(early)
     select, gate_column = route(at, pieces[:middle] + [far_info] + pieces[middle + 1 :], wide)
     rows = pack(select, gate_column, pieces, first, second)
@@ -471,11 +504,10 @@
     rows = rows.reshape(slot_total, wide + LANES)
 
     early = settle(at, crossed)
-    acc = jnp.dot(early, weight_own[rest:], preferred_element_type=f32)
-    grad_hidden, gate_grad, gated = back(rows, acc, hidden, weight_other, weight_own, rest)
+    grad_hidden, gate_grad, gated = back(rows, early, hidden, weight_other, weight_own)
     grad_hidden = grad_hidden.reshape(saved_hidden.shape)
     returned = lax.all_to_all(
-        gate_grad.reshape(experts, CAP),
+        gate_grad[:, :CAP],
         ("node", "local"),
         split_axis=0,
         concat_axis=0,
@@ -485,8 +517,8 @@
         rows[:, :half], gated, (((0,), (0,)), ((), ())), preferred_element_type=f32
     )
     received = lax.ppermute(received.astype(bf16), "replica", swap)
-    grad_down = down(rows[:, half:wide], 0, early, gated, received)
-    grad_logits = finish(info, router_logits.T, returned, (grad_down,)).T
+    grad_down, mark = down(rows, half, early, gated, received)
+    grad_logits = finish(info, router_logits.T, returned, (mark,)).T
     return (grad_logits, grad_hidden, grad_down.reshape(down_weight.shape))
 
 

time: 201 us -> 191 us (0.950)
  waiting for transfers between devices: 60.4 us -> 52.9 us
  starting transfers between devices: 71 us -> 77.2 us
  matrix products: 11.7 us -> 6.3 us
  local copies, waits for them, and re-layouts: 9.54 us -> 4.27 us
  Pallas kernels: 41.9 us -> 46.8 us
  other arithmetic: 4.57 us -> 1.28 us
    ppermute x3, waiting for transfers between devices: 32 us -> 3.14 us  [ring(): up = lax.ppermute(up, 'local', ahead)]
    ppermute x3, waiting for transfers between devices: 0.01 us -> 25.3 us  [ring(): down = lax.ppermute(down, 'local', back)]
    ppermute x8, waiting for transfers between devices: 27.4 us -> 21.2 us  [step(): return lax.ppermute(x, 'local', [(i, (i + k) % RING) for i in range(RING)])]
    dot_general x1 -> x0, matrix products: 4.66 us -> none  [local(): acc = jnp.dot(early, weight_own[rest:], preferred_element_type=f32)]
    ppermute x3, starting transfers between devices: 9.37 us -> 13.4 us  [ring(): down = lax.ppermute(down, 'local', back)]
    all_to_all x1, starting transfers between devices: 12 us -> 15.6 us  [local(): lax.all_to_all(gate_grad[:, :CAP], ('node', 'local'), split_axis=0, conca...]
    ppermute x8, starting transfers between devices: 16.5 us -> 20.1 us  [step(): return lax.ppermute(x, 'local', [(i, (i + k) % RING) for i in range(RING)])]
    unnamed x42 -> x16, local copies, waits for them, and re-layouts: 7.39 us -> 4.22 us
  transfers between devices with their start and end apart: 22 -> 22, of which waited for: 9 -> 12; matrix products, arithmetic and copies ran while one was open for 4% -> 0% of each run, Pallas kernels for 14% -> 18%
where the time goes in v2:
time: 191 us; the launch traced here: 190 us
  starting transfers between devices  77.2 us (40%)
  waiting for transfers between devices  52.9 us (28%)
  Pallas kernels  46.8 us (25%)
  matrix products  6.3 us (3%)
  local copies, waits for them, and re-layouts  4.27 us (2%)
    ppermute x3, waiting for transfers between devices, ring(): down = lax.ppermute(down, 'local', back)  25.3 us
    ppermute x8, waiting for transfers between devices, step(): return lax.ppermute(x, 'local', [(i, (i + k) % RING) for i in range(RING)])  21.2 us
    ppermute x8, starting transfers between devices, step(): return lax.ppermute(x, 'local', [(i, (i + k) % RING) for i in range(RING)])  20.1 us
    all_to_all x1, starting transfers between devices, local(): lax.all_to_all(gate_grad[:, :CAP], ('node', 'local'), split_axis=0, conca...  15.6 us
    ppermute x3, starting transfers between devices, ring(): down = lax.ppermute(down, 'local', back)  13.4 us
    pallas_call x1, Pallas kernels, back(): pl.pallas_call(functools.partial(back_kernel, half - early.shape[1]), gri...  10.6 us
    pallas_call x1, Pallas kernels, pack(): pl.pallas_call(functools.partial(pack_kernel, halfway), grid=(2 * halfway...  9.47 us
    pallas_call x1, Pallas kernels, down(): pl.pallas_call(functools.partial(down_kernel, steps), grid=(steps + more,...  8.27 us
  transfers between devices with their start and end apart: 22, of which 12 were waited for; matrix products, arithmetic and copies ran while one was open for 0% of the time, Pallas kernels for 18%

profile of v2, /device:TPU:1, one launch (start us, length us, event | category | flops | bytes accessed | tf_op | source)
XLA Modules:
  0.0 189.7 jit_solution(15551291334518200329)
XLA Ops:
  2.1 6.5 %collective-permute-start.4 = (bf16[128,2432]{1,0:T(8,128)(2,1)S(1)}, bf16[128,2432]{1,0:T(8,128)(2,1)S(1)}, u32[]{:S(2)}, u32[]{:S(2)}) collective-permute-start(bf16[128,2432]{1,0:T(8,128)(2,1)S(1)} %pad_maximum_fusion.refs_0_), channel_id=1, source_target_pairs={{0,14},{2,0},{4,2},{6,4},{8,6},{10,8},{12,10},{14,12},{1,15},{3,1}... | collective-permute-start | bytes 1867784 | tf_op jit(solution)/shard_map/ppermute | solution.py:330
  8.6 12.7 %collective-permute-done.4.refs_7_.refs_6_ = bf16[128,2432]{1,0:T(8,128)(2,1)S(1)} collective-permute-done((bf16[128,2432]{1,0:T(8,128)(2,1)S(1)}, bf16[128,2432]{1,0:T(8,128)(2,1)S(1)}, u32[]{:S(2)}, u32[]{:S(2)}) %collective-permute-start.4) | collective-permute-done | bytes 622624 | tf_op jit(solution)/shard_map/ppermute | solution.py:330
  21.3 3.4 %collective-permute-start.5 = (bf16[128,2432]{1,0:T(8,128)(2,1)S(1)}, bf16[128,2432]{1,0:T(8,128)(2,1)}, u32[]{:S(2)}, u32[]{:S(2)}) collective-permute-start(bf16[128,2432]{1,0:T(8,128)(2,1)S(1)} %collective-permute-done.4.refs_7_.refs_6_), channel_id=1, source_target_pairs={{0,14},{2,0},{4,2},{6,4},{8,6},{10,8},{12,10},{14,12},{1,15},{3,1}... | collective-permute-start | bytes 1867784 | tf_op jit(solution)/shard_map/ppermute | solution.py:330
  24.8 3.5 %own_slots.1 = bf16[768,1280]{1,0:T(8,128)(2,1)} custom-call(bf16[128,128]{1,0:T(8,128)(2,1)S(1)} %codes.1.info_ref, bf16[128,1280]{1,0:T(8,128)(2,1)S(1)} %slice.33.x_ref), custom_call_target="tpu_custom_call" | custom-call | flops 251658240 | bytes 1966080 | tf_op jit(solution)/shard_map/own_slots/pallas_call | solution.py:188
  28.2 6.8 %all-to-all-start.1 = ((bf16[16,48,1280]{2,1,0:T(8,128)(2,1)}), bf16[16,48,1280]{2,1,0:T(8,128)(2,1)}, u32[]{:S(2)}, u32[]{:S(2)}) async-start(bf16[16,48,1280]{2,1,0:T(8,128)(2,1)} %bitcast.6), calls=%async_computation.1 | async-start | bytes 3932160 | tf_op jit(solution)/shard_map/all_to_all | solution.py:496
  36.5 3.5 %collective-permute-start.6 = (bf16[128,2432]{1,0:T(8,128)(2,1)}, bf16[128,2432]{1,0:T(8,128)(2,1)S(1)}, u32[]{:S(2)}, u32[]{:S(2)}) collective-permute-start(bf16[128,2432]{1,0:T(8,128)(2,1)} %collective-permute-done.5.refs_6_.refs_5_), channel_id=1, source_target_pairs={{0,14},{2,0},{4,2},{6,4},{8,6},{10,8},{12,10},{14,12},{1,15},{3,1}... | collective-permute-start | bytes 1867784 | tf_op jit(solution)/shard_map/ppermute | solution.py:330
  40.0 11.2 %collective-permute-done.6.refs_5_.down_ref.refs_4_ = bf16[128,2432]{1,0:T(8,128)(2,1)S(1)} collective-permute-done((bf16[128,2432]{1,0:T(8,128)(2,1)}, bf16[128,2432]{1,0:T(8,128)(2,1)S(1)}, u32[]{:S(2)}, u32[]{:S(2)}) %collective-permute-start.6) | collective-permute-done | bytes 622624 | tf_op jit(solution)/shard_map/ppermute | solution.py:330
  60.5 4.2 %collective-permute-start.17 = (bf16[1792,1024]{1,0:T(8,128)(2,1)}, bf16[1792,1024]{1,0:T(8,128)(2,1)}, u32[]{:S(2)}, u32[]{:S(2)}) collective-permute-start(bf16[1792,1024]{1,0:T(8,128)(2,1)} %bitcast.24), channel_id=1, source_target_pairs={{0,1},{1,0},{2,3},{3,2},{4,5},{5,4},{6,7},{7,6},{8,9},{9,8},{10,11... | collective-permute-start | bytes 11010056 | tf_op jit(solution)/shard_map/ppermute | solution.py:481
  65.6 3.3 %route.1 = (bf16[768,1024]{1,0:T(8,128)(2,1)S(1)}, bf16[768,128]{1,0:T(8,128)(2,1)S(1)}) custom-call(s32[1]{0:T(128)} %bitcast.3.z_ref, bf16[128,2432]{1,0:T(8,128)(2,1)S(1)} %pad_maximum_fusion.refs_0_, bf16[128,2432]{1,0:T(8,128)(2,1)S(1)} %collective-permute-done.refs_1_, bf16[128,2432]{1,0:T(8,128)(2,1)} %collective-permute-done.1.refs_2_, ...), custom_call_target="tpu_custom_call" | custom-call | flops 100000000 | bytes 2000000 | tf_op jit(solution)/shard_map/route/pallas_call | solution.py:91
  69.0 9.5 %pack.1 = bf16[768,2432]{1,0:T(8,128)(2,1)} custom-call(bf16[768,1024]{1,0:T(8,128)(2,1)S(1)} %get-tuple-element.19.select_ref, bf16[768,128]{1,0:T(8,128)(2,1)S(1)} %get-tuple-element.20.gate_ref, bf16[128,2432]{1,0:T(8,128)(2,1)S(1)} %pad_maximum_fusion.refs_0_, bf16[128,2432]{1,0:T(8,128)(2,1)S(1)} %collective-permute-done.refs_1_, ...), custom_call_target="tpu_custom_call" | custom-call | flops 3623878656 | bytes 9830400 | tf_op jit(solution)/shard_map/pack/pallas_call | solution.py:129
  78.4 6.7 %all-to-all-start = ((bf16[16,48,2432]{2,1,0:T(8,128)(2,1)}), bf16[16,48,2432]{2,1,0:T(8,128)(2,1)}, u32[]{:S(2)}, u32[]{:S(2)}) async-start(bf16[16,48,2432]{2,1,0:T(8,128)(2,1)} %bitcast.27), calls=%async_computation | async-start | bytes 7471104 | tf_op jit(solution)/shard_map/all_to_all | solution.py:503
  85.2 5.4 %turn.1 = (bf16[96,1280]{1,0:T(8,128)(2,1)S(1)}, bf16[96,1280]{1,0:T(8,128)(2,1)S(1)}, bf16[144,1280]{1,0:T(8,128)(2,1)S(1)}, bf16[96,1280]{1,0:T(8,128)(2,1)S(1...) custom-call(s32[1]{0:T(128)} %bitcast.3.z_ref, ...), custom_call_target="tpu_custom_call" | custom-call | flops 1509949440 | bytes 3932160 | tf_op jit(solution)/shard_map/turn/pallas_call | solution.py:236
  90.6 3.6 %collective-permute-start.13 = (bf16[144,1280]{1,0:T(8,128)(2,1)S(1)}, bf16[144,1280]{1,0:T(8,128)(2,1)S(1)}, u32[]{:S(2)}, u32[]{:S(2)}) collective-permute-start(bf16[144,1280]{1,0:T(8,128)(2,1)S(1)} %get-tuple-element.27), channel_id=1, source_target_pairs={{0,12},{2,14},{4,0},{6,2},{8,4},{10,6},{12,8},{14,10},{1,13},{3,15... | collective-permute-start | bytes 1105928 | tf_op jit(solution)/shard_map/ppermute | solution.py:256
  97.2 7.0 %collective-permute-done.10.refs_2_ = bf16[144,1280]{1,0:T(8,128)(2,1)S(1)} collective-permute-done((bf16[144,1280]{1,0:T(8,128)(2,1)S(1)}, bf16[144,1280]{1,0:T(8,128)(2,1)S(1)}, u32[]{:S(2)}, u32[]{:S(2)}) %collective-permute-start.10) | collective-permute-done | bytes 368672 | tf_op jit(solution)/shard_map/ppermute | solution.py:256
  109.7 6.1 %collective-permute-start.12 = (bf16[48,1280]{1,0:T(8,128)(2,1)S(1)}, bf16[48,1280]{1,0:T(8,128)(2,1)S(1)}, u32[]{:S(2)}, u32[]{:S(2)}) collective-permute-start(bf16[48,1280]{1,0:T(8,128)(2,1)S(1)} %slice.34), channel_id=1, source_target_pairs={{0,4},{2,6},{4,8},{6,10},{8,12},{10,14},{12,0},{14,2},{1,5},{3,7},... | collective-permute-start | bytes 368648 | tf_op jit(solution)/shard_map/ppermute | solution.py:256
  115.9 5.2 %collective-permute-done.11.refs_3_ = bf16[96,1280]{1,0:T(8,128)(2,1)S(1)} collective-permute-done((bf16[96,1280]{1,0:T(8,128)(2,1)S(1)}, bf16[96,1280]{1,0:T(8,128)(2,1)S(1)}, u32[]{:S(2)}, u32[]{:S(2)}) %collective-permute-start.11) | collective-permute-done | bytes 245792 | tf_op jit(solution)/shard_map/ppermute | solution.py:256
  121.1 4.2 %collective-permute-start.14 = (bf16[48,1280]{1,0:T(8,128)(2,1)S(1)}, bf16[48,1280]{1,0:T(8,128)(2,1)S(1)}, u32[]{:S(2)}, u32[]{:S(2)}) collective-permute-start(bf16[48,1280]{1,0:T(8,128)(2,1)S(1)} %slice.35), channel_id=1, source_target_pairs={{0,12},{2,14},{4,0},{6,2},{8,4},{10,6},{12,8},{14,10},{1,13},{3,15... | collective-permute-start | bytes 368648 | tf_op jit(solution)/shard_map/ppermute | solution.py:256
  125.3 3.3 %collective-permute-done.16.refs_8_ = bf16[96,1280]{1,0:T(8,128)(2,1)S(1)} collective-permute-done((bf16[96,1280]{1,0:T(8,128)(2,1)S(1)}, bf16[96,1280]{1,0:T(8,128)(2,1)S(1)}, u32[]{:S(2)}, u32[]{:S(2)}) %collective-permute-start.16) | collective-permute-done | bytes 245792 | tf_op jit(solution)/shard_map/ppermute | solution.py:256
  128.5 3.3 %collective-permute-done.12.refs_4_ = bf16[48,1280]{1,0:T(8,128)(2,1)S(1)} collective-permute-done((bf16[48,1280]{1,0:T(8,128)(2,1)S(1)}, bf16[48,1280]{1,0:T(8,128)(2,1)S(1)}, u32[]{:S(2)}, u32[]{:S(2)}) %collective-permute-start.12) | collective-permute-done | bytes 122912 | tf_op jit(solution)/shard_map/ppermute | solution.py:256
  138.4 10.6 %back.1 = (bf16[768,1024]{1,0:T(8,128)(2,1)}, f32[128,128]{1,0:T(8,128)S(1)}, bf16[768,1024]{1,0:T(8,128)(2,1)S(1)}) custom-call(bf16[768,2432]{1,0:T(8,128)(2,1)} %bitcast.5.rows_ref.x_ref, bf16[768,1280]{1,0:T(8,128)(2,1)S(1)} %settle.1.early_ref.y_ref, bf16[768,1024]{1,0:T(8,128)(2,1)S(1)} %bitcast.26, ...), custom_call_target="tpu_custom_call" | custom-call | flops 5637144576 | bytes 18000000 | tf_op jit(solution)/shard_map/back/pallas_call | solution.py:371
  148.9 6.3 %convolution_convert_fusion = bf16[1792,1024]{1,0:T(8,128)(2,1)} fusion(bf16[768,1024]{1,0:T(8,128)(2,1)S(1)} %get-tuple-element.31.gated_ref, bf16[768,2432]{1,0:T(8,128)(2,1)} %bitcast.5.rows_ref.x_ref), kind=kOutput, calls=%fused_computation | convolution fusion | flops 2820407296 | bytes 7995392 | tf_op jit(solution)/shard_map/dot_general | solution.py:516
  155.2 5.8 %collective-permute-start.18 = (bf16[1792,1024]{1,0:T(8,128)(2,1)}, bf16[1792,1024]{1,0:T(8,128)(2,1)}, u32[]{:S(2)}, u32[]{:S(2)}) collective-permute-start(bf16[1792,1024]{1,0:T(8,128)(2,1)} %convolution_convert_fusion), channel_id=1, source_target_pairs={{0,1},{1,0},{2,3},{3,2},{4,5},{5,4},{6,7},{7,6},{8,9},{9,8},{10,11... | collective-permute-start | bytes 11010056 | tf_op jit(solution)/shard_map/ppermute | solution.py:519
  161.0 15.6 %all-to-all-start.2 = ((f32[128,1,6]{2,1,0:T(1,128)}), f32[128,1,6]{2,1,0:T(1,128)}, u32[]{:S(2)}, u32[]{:S(2)}) async-start(f32[128,1,6]{2,1,0:T(1,128)} %bitcast.19), calls=%async_computation.2 | async-start | bytes 131072 | tf_op jit(solution)/shard_map/all_to_all | solution.py:509
  176.6 8.3 %down.1 = (bf16[1792,1024]{1,0:T(8,128)(2,1)}, f32[8,128]{1,0:T(8,128)S(1)}) custom-call(bf16[768,2432]{1,0:T(8,128)(2,1)} %bitcast.5.rows_ref.x_ref, bf16[768,1280]{1,0:T(8,128)(2,1)S(1)} %settle.1.early_ref.y_ref, bf16[768,1024]{1,0:T(8,128)(2,1)S(1)} %get-tuple-element.31.gated_ref, bf16[1792,1024]{1,0:T(8,128)(2,1)} %collective-permute-done.18.received_ref), custom_call_target="tpu_custom_call" | custom-call | flops 2818572288 | bytes 12000000 | tf_op jit(solution)/shard_map/down/pallas_call | solution.py:412
  (53 shorter events, 33.1 us)
Async XLA Ops:
  2.1 56.5 %copy-start = (bf16[128,128]{1,0:T(8,128)(2,1)}, bf16[128,128]{1,0:T(8,128)(2,1)S(1)}, u32[]{:S(2)}) copy-start(bf16[128,128]{1,0:T(8,128)(2,1)S(1)} %codes.1.info_ref) | copy-start | bytes 98308
  2.1 19.2 %collective-permute-start.4 = (bf16[128,2432]{1,0:T(8,128)(2,1)S(1)}, bf16[128,2432]{1,0:T(8,128)(2,1)S(1)}, u32[]{:S(2)}, u32[]{:S(2)}) collective-permute-start(bf16[128,2432]{1,0:T(8,128)(2,1)S(1)} %pad_maximum_fusion.refs_0_), channel_id=1, source_target_pairs={{0,14},{2,0},{4,2},{6,4},{8,6},{10,8},{12,10},{14,12},{1,15},{3,1}... | collective-permute-start | bytes 1867784 | tf_op jit(solution)/shard_map/ppermute | solution.py:330
  8.6 16.1 %collective-permute-start = (bf16[128,2432]{1,0:T(8,128)(2,1)S(1)}, bf16[128,2432]{1,0:T(8,128)(2,1)S(1)}, u32[]{:S(2)}, u32[]{:S(2)}) collective-permute-start(bf16[128,2432]{1,0:T(8,128)(2,1)S(1)} %pad_maximum_fusion.refs_0_), channel_id=1, source_target_pairs={{0,2},{2,4},{4,6},{6,8},{8,10},{10,12},{12,14},{14,0},{1,3},{3,5},... | collective-permute-start | bytes 1867784 | tf_op jit(solution)/shard_map/ppermute | solution.py:329
  21.3 15.2 %collective-permute-start.5 = (bf16[128,2432]{1,0:T(8,128)(2,1)S(1)}, bf16[128,2432]{1,0:T(8,128)(2,1)}, u32[]{:S(2)}, u32[]{:S(2)}) collective-permute-start(bf16[128,2432]{1,0:T(8,128)(2,1)S(1)} %collective-permute-done.4.refs_7_.refs_6_), channel_id=1, source_target_pairs={{0,14},{2,0},{4,2},{6,4},{8,6},{10,8},{12,10},{14,12},{1,15},{3,1}... | collective-permute-start | bytes 1867784 | tf_op jit(solution)/shard_map/ppermute | solution.py:330
  24.7 15.3 %collective-permute-start.1 = (bf16[128,2432]{1,0:T(8,128)(2,1)S(1)}, bf16[128,2432]{1,0:T(8,128)(2,1)}, u32[]{:S(2)}, u32[]{:S(2)}) collective-permute-start(bf16[128,2432]{1,0:T(8,128)(2,1)S(1)} %collective-permute-done.refs_1_), channel_id=1, source_target_pairs={{0,2},{2,4},{4,6},{6,8},{8,10},{10,12},{12,14},{14,0},{1,3},{3,5},... | collective-permute-start | bytes 1867784 | tf_op jit(solution)/shard_map/ppermute | solution.py:329
  28.2 50.2 %all-to-all-start.1 = ((bf16[16,48,1280]{2,1,0:T(8,128)(2,1)}), bf16[16,48,1280]{2,1,0:T(8,128)(2,1)}, u32[]{:S(2)}, u32[]{:S(2)}) async-start(bf16[16,48,1280]{2,1,0:T(8,128)(2,1)} %bitcast.6), calls=%async_computation.1 | async-start | bytes 3932160 | tf_op jit(solution)/shard_map/all_to_all | solution.py:496
  36.5 14.7 %collective-permute-start.6 = (bf16[128,2432]{1,0:T(8,128)(2,1)}, bf16[128,2432]{1,0:T(8,128)(2,1)S(1)}, u32[]{:S(2)}, u32[]{:S(2)}) collective-permute-start(bf16[128,2432]{1,0:T(8,128)(2,1)} %collective-permute-done.5.refs_6_.refs_5_), channel_id=1, source_target_pairs={{0,14},{2,0},{4,2},{6,4},{8,6},{10,8},{12,10},{14,12},{1,15},{3,1}... | collective-permute-start | bytes 1867784 | tf_op jit(solution)/shard_map/ppermute | solution.py:330
  40.0 14.3 %collective-permute-start.2 = (bf16[128,2432]{1,0:T(8,128)(2,1)}, bf16[128,2432]{1,0:T(8,128)(2,1)S(1)}, u32[]{:S(2)}, u32[]{:S(2)}) collective-permute-start(bf16[128,2432]{1,0:T(8,128)(2,1)} %collective-permute-done.1.refs_2_), channel_id=1, source_target_pairs={{0,2},{2,4},{4,6},{6,8},{8,10},{10,12},{12,14},{14,0},{1,3},{3,5},... | collective-permute-start | bytes 1867784 | tf_op jit(solution)/shard_map/ppermute | solution.py:329
  55.9 13.1 %collective-permute-start.7 = (bf16[128,1152]{1,0:T(8,128)(2,1)}, bf16[128,1152]{1,0:T(8,128)(2,1)S(1)}, u32[]{:S(2)}, u32[]{:S(2)}) collective-permute-start(bf16[128,1152]{1,0:T(8,128)(2,1)} %get-tuple-element.21), channel_id=1, source_target_pairs={{0,2},{2,4},{4,6},{6,8},{8,10},{10,12},{12,14},{14,0},{1,3},{3,5},... | collective-permute-start | bytes 884744 | tf_op jit(solution)/shard_map/ppermute | solution.py:339
  55.9 13.1 %collective-permute-start.8 = (bf16[128,1152]{1,0:T(8,128)(2,1)}, bf16[128,1152]{1,0:T(8,128)(2,1)}, u32[]{:S(2)}, u32[]{:S(2)}) collective-permute-start(bf16[128,1152]{1,0:T(8,128)(2,1)} %get-tuple-element.22), channel_id=1, source_target_pairs={{0,14},{2,0},{4,2},{6,4},{8,6},{10,8},{12,10},{14,12},{1,15},{3,1}... | collective-permute-start | bytes 884744 | tf_op jit(solution)/shard_map/ppermute | solution.py:339
  58.5 7.1 %collective-permute-start.3 = (bf16[128,128]{1,0:T(8,128)(2,1)S(1)}, bf16[128,128]{1,0:T(8,128)(2,1)S(1)}, u32[]{:S(2)}, u32[]{:S(2)}) collective-permute-start(bf16[128,128]{1,0:T(8,128)(2,1)S(1)} %codes.1.info_ref), channel_id=1, source_target_pairs={{0,8},{2,10},{4,12},{6,14},{8,0},{10,2},{12,4},{14,6},{1,9},{3,11}... | collective-permute-start | bytes 98312 | tf_op jit(solution)/shard_map/ppermute | solution.py:492
  60.5 74.4 %collective-permute-start.17 = (bf16[1792,1024]{1,0:T(8,128)(2,1)}, bf16[1792,1024]{1,0:T(8,128)(2,1)}, u32[]{:S(2)}, u32[]{:S(2)}) collective-permute-start(bf16[1792,1024]{1,0:T(8,128)(2,1)} %bitcast.24), channel_id=1, source_target_pairs={{0,1},{1,0},{2,3},{3,2},{4,5},{5,4},{6,7},{7,6},{8,9},{9,8},{10,11... | collective-permute-start | bytes 11010056 | tf_op jit(solution)/shard_map/ppermute | solution.py:481
  78.4 56.5 %all-to-all-start = ((bf16[16,48,2432]{2,1,0:T(8,128)(2,1)}), bf16[16,48,2432]{2,1,0:T(8,128)(2,1)}, u32[]{:S(2)}, u32[]{:S(2)}) async-start(bf16[16,48,2432]{2,1,0:T(8,128)(2,1)} %bitcast.27), calls=%async_computation | async-start | bytes 7471104 | tf_op jit(solution)/shard_map/all_to_all | solution.py:503
  90.5 13.7 %collective-permute-start.10 = (bf16[144,1280]{1,0:T(8,128)(2,1)S(1)}, bf16[144,1280]{1,0:T(8,128)(2,1)S(1)}, u32[]{:S(2)}, u32[]{:S(2)}) collective-permute-start(bf16[144,1280]{1,0:T(8,128)(2,1)S(1)} %get-tuple-element.25), channel_id=1, source_target_pairs={{0,4},{2,6},{4,8},{6,10},{8,12},{10,14},{12,0},{14,2},{1,5},{3,7},... | collective-permute-start | bytes 1105928 | tf_op jit(solution)/shard_map/ppermute | solution.py:256
  90.6 15.3 %collective-permute-start.13 = (bf16[144,1280]{1,0:T(8,128)(2,1)S(1)}, bf16[144,1280]{1,0:T(8,128)(2,1)S(1)}, u32[]{:S(2)}, u32[]{:S(2)}) collective-permute-start(bf16[144,1280]{1,0:T(8,128)(2,1)S(1)} %get-tuple-element.27), channel_id=1, source_target_pairs={{0,12},{2,14},{4,0},{6,2},{8,4},{10,6},{12,8},{14,10},{1,13},{3,15... | collective-permute-start | bytes 1105928 | tf_op jit(solution)/shard_map/ppermute | solution.py:256
  94.2 15.6 %collective-permute-start.9 = (bf16[96,1280]{1,0:T(8,128)(2,1)S(1)}, bf16[96,1280]{1,0:T(8,128)(2,1)S(1)}, u32[]{:S(2)}, u32[]{:S(2)}) collective-permute-start(bf16[96,1280]{1,0:T(8,128)(2,1)S(1)} %get-tuple-element.24), channel_id=1, source_target_pairs={{0,2},{2,4},{4,6},{6,8},{8,10},{10,12},{12,14},{14,0},{1,3},{3,5},... | collective-permute-start | bytes 737288 | tf_op jit(solution)/shard_map/ppermute | solution.py:256
  94.2 26.9 %collective-permute-start.11 = (bf16[96,1280]{1,0:T(8,128)(2,1)S(1)}, bf16[96,1280]{1,0:T(8,128)(2,1)S(1)}, u32[]{:S(2)}, u32[]{:S(2)}) collective-permute-start(bf16[96,1280]{1,0:T(8,128)(2,1)S(1)} %get-tuple-element.26), channel_id=1, source_target_pairs={{0,6},{2,8},{4,10},{6,12},{8,14},{10,0},{12,2},{14,4},{1,7},{3,9},... | collective-permute-start | bytes 737288 | tf_op jit(solution)/shard_map/ppermute | solution.py:256
  104.2 21.1 %collective-permute-start.15 = (bf16[96,1280]{1,0:T(8,128)(2,1)S(1)}, bf16[96,1280]{1,0:T(8,128)(2,1)S(1)}, u32[]{:S(2)}, u32[]{:S(2)}) collective-permute-start(bf16[96,1280]{1,0:T(8,128)(2,1)S(1)} %get-tuple-element.28), channel_id=1, source_target_pairs={{0,10},{2,12},{4,14},{6,0},{8,2},{10,4},{12,6},{14,8},{1,11},{3,13... | collective-permute-start | bytes 737288 | tf_op jit(solution)/shard_map/ppermute | solution.py:256
  105.9 22.6 %collective-permute-start.16 = (bf16[96,1280]{1,0:T(8,128)(2,1)S(1)}, bf16[96,1280]{1,0:T(8,128)(2,1)S(1)}, u32[]{:S(2)}, u32[]{:S(2)}) collective-permute-start(bf16[96,1280]{1,0:T(8,128)(2,1)S(1)} %get-tuple-element.29), channel_id=1, source_target_pairs={{0,14},{2,0},{4,2},{6,4},{8,6},{10,8},{12,10},{14,12},{1,15},{3,1}... | collective-permute-start | bytes 737288 | tf_op jit(solution)/shard_map/ppermute | solution.py:256
  109.7 22.1 %collective-permute-start.12 = (bf16[48,1280]{1,0:T(8,128)(2,1)S(1)}, bf16[48,1280]{1,0:T(8,128)(2,1)S(1)}, u32[]{:S(2)}, u32[]{:S(2)}) collective-permute-start(bf16[48,1280]{1,0:T(8,128)(2,1)S(1)} %slice.34), channel_id=1, source_target_pairs={{0,4},{2,6},{4,8},{6,10},{8,12},{10,14},{12,0},{14,2},{1,5},{3,7},... | collective-permute-start | bytes 368648 | tf_op jit(solution)/shard_map/ppermute | solution.py:256
  121.1 10.8 %collective-permute-start.14 = (bf16[48,1280]{1,0:T(8,128)(2,1)S(1)}, bf16[48,1280]{1,0:T(8,128)(2,1)S(1)}, u32[]{:S(2)}, u32[]{:S(2)}) collective-permute-start(bf16[48,1280]{1,0:T(8,128)(2,1)S(1)} %slice.35), channel_id=1, source_target_pairs={{0,12},{2,14},{4,0},{6,2},{8,4},{10,6},{12,8},{14,10},{1,13},{3,15... | collective-permute-start | bytes 368648 | tf_op jit(solution)/shard_map/ppermute | solution.py:256
  148.9 6.3 %copy-start.2 = (f32[128,128]{1,0:T(8,128)}, f32[128,128]{1,0:T(8,128)S(1)}, u32[]{:S(2)}) copy-start(f32[128,128]{1,0:T(8,128)S(1)} %get-tuple-element.30) | copy-start | bytes 196612
  155.2 21.4 %collective-permute-start.18 = (bf16[1792,1024]{1,0:T(8,128)(2,1)}, bf16[1792,1024]{1,0:T(8,128)(2,1)}, u32[]{:S(2)}, u32[]{:S(2)}) collective-permute-start(bf16[1792,1024]{1,0:T(8,128)(2,1)} %convolution_convert_fusion), channel_id=1, source_target_pairs={{0,1},{1,0},{2,3},{3,2},{4,5},{5,4},{6,7},{7,6},{8,9},{9,8},{10,11... | collective-permute-start | bytes 11010056 | tf_op jit(solution)/shard_map/ppermute | solution.py:519
  161.0 26.2 %all-to-all-start.2 = ((f32[128,1,6]{2,1,0:T(1,128)}), f32[128,1,6]{2,1,0:T(1,128)}, u32[]{:S(2)}, u32[]{:S(2)}) async-start(f32[128,1,6]{2,1,0:T(1,128)} %bitcast.19), calls=%async_computation.2 | async-start | bytes 131072 | tf_op jit(solution)/shard_map/all_to_all | solution.py:509
  (6 other events, 8.1 us)

commit v3 on v2

--- a/solution.py
+++ b/solution.py
@@ -495,7 +495,7 @@
     early = early.reshape(NODES, BLOCK, EARLY)
     early = lax.all_to_all(early, "node", split_axis=0, concat_axis=0, tiled=True)
     early = turn(at, early.reshape(slot_total, EARLY))
-    first, second = farthest(pieces[middle - 1], pieces[middle + 1], ())
+    first, second = farthest(pieces[middle - 1], pieces[middle + 1], (far_info,))
     crossed = cross(early)
     select, gate_column = route(at, pieces[:middle] + [far_info] + pieces[middle + 1 :], wide)
     rows = pack(select, gate_column, pieces, first, second)

time: 191 us -> 187 us (0.979)
  starting transfers between devices: 77.2 us -> 69.3 us
  waiting for transfers between devices: 52.9 us -> 57.8 us
    ppermute x1, waiting for transfers between devices: 0.94 us -> 12.4 us  [local(): lax.ppermute(info, 'local', [(i, (i + middle) % RING) for i in range(RING)])]
    ppermute x3, waiting for transfers between devices: 25.3 us -> 14.2 us  [ring(): down = lax.ppermute(down, 'local', back)]
    ppermute x8, waiting for transfers between devices: 21.2 us -> 28.1 us  [step(): return lax.ppermute(x, 'local', [(i, (i + k) % RING) for i in range(RING)])]
    ppermute x1, starting transfers between devices: 5.78 us -> 1.56 us  [local(): received = lax.ppermute(received.astype(bf16), 'replica', swap)]
    ppermute x8, starting transfers between devices: 20.1 us -> 17.7 us  [step(): return lax.ppermute(x, 'local', [(i, (i + k) % RING) for i in range(RING)])]
    ppermute x3, waiting for transfers between devices: 3.14 us -> 0.74 us  [ring(): up = lax.ppermute(up, 'local', ahead)]
  transfers between devices with their start and end apart: 22 -> 22, of which waited for: 12 -> 10; matrix products, arithmetic and copies ran while one was open for 0% -> 0% of each run, Pallas kernels for 18% -> 18%
where the time goes in v3:
time: 187 us
  starting transfers between devices  69.3 us (37%)
  waiting for transfers between devices  57.8 us (31%)
  Pallas kernels  46.8 us (25%)
  matrix products  6.3 us (3%)
  local copies, waits for them, and re-layouts  4.27 us (2%)
    ppermute x8, waiting for transfers between devices, step(): return lax.ppermute(x, 'local', [(i, (i + k) % RING) for i in range(RING)])  28.1 us
    ppermute x8, starting transfers between devices, step(): return lax.ppermute(x, 'local', [(i, (i + k) % RING) for i in range(RING)])  17.7 us
    ppermute x3, waiting for transfers between devices, ring(): down = lax.ppermute(down, 'local', back)  14.2 us
    all_to_all x1, starting transfers between devices, local(): lax.all_to_all(gate_grad[:, :CAP], ('node', 'local'), split_axis=0, conca...  13.7 us
    ppermute x3, starting transfers between devices, ring(): down = lax.ppermute(down, 'local', back)  13.4 us
    ppermute x1, waiting for transfers between devices, local(): lax.ppermute(info, 'local', [(i, (i + middle) % RING) for i in range(RING)])  12.4 us
    pallas_call x1, Pallas kernels, back(): pl.pallas_call(functools.partial(back_kernel, half - early.shape[1]), gri...  10.6 us
    pallas_call x1, Pallas kernels, pack(): pl.pallas_call(functools.partial(pack_kernel, halfway), grid=(2 * halfway...  9.48 us
  transfers between devices with their start and end apart: 22, of which 10 were waited for; matrix products, arithmetic and copies ran while one was open for 0% of the time, Pallas kernels for 18%

profile of v3, /device:TPU:1, one launch (start us, length us, event | category | flops | bytes accessed | tf_op | source)
XLA Modules:
  0.0 186.7 jit_solution(12715257389660453385)
XLA Ops:
  2.1 6.5 %collective-permute-start.4 = (bf16[128,2432]{1,0:T(8,128)(2,1)S(1)}, bf16[128,2432]{1,0:T(8,128)(2,1)S(1)}, u32[]{:S(2)}, u32[]{:S(2)}) collective-permute-start(bf16[128,2432]{1,0:T(8,128)(2,1)S(1)} %pad_maximum_fusion.refs_0_), channel_id=1, source_target_pairs={{0,14},{2,0},{4,2},{6,4},{8,6},{10,8},{12,10},{14,12},{1,15},{3,1}... | collective-permute-start | bytes 1867784 | tf_op jit(solution)/shard_map/ppermute | solution.py:330
  8.6 12.7 %collective-permute-done.4.refs_7_.refs_6_ = bf16[128,2432]{1,0:T(8,128)(2,1)S(1)} collective-permute-done((bf16[128,2432]{1,0:T(8,128)(2,1)S(1)}, bf16[128,2432]{1,0:T(8,128)(2,1)S(1)}, u32[]{:S(2)}, u32[]{:S(2)}) %collective-permute-start.4) | collective-permute-done | bytes 622624 | tf_op jit(solution)/shard_map/ppermute | solution.py:330
  21.3 3.4 %collective-permute-start.5 = (bf16[128,2432]{1,0:T(8,128)(2,1)S(1)}, bf16[128,2432]{1,0:T(8,128)(2,1)}, u32[]{:S(2)}, u32[]{:S(2)}) collective-permute-start(bf16[128,2432]{1,0:T(8,128)(2,1)S(1)} %collective-permute-done.4.refs_7_.refs_6_), channel_id=1, source_target_pairs={{0,14},{2,0},{4,2},{6,4},{8,6},{10,8},{12,10},{14,12},{1,15},{3,1}... | collective-permute-start | bytes 1867784 | tf_op jit(solution)/shard_map/ppermute | solution.py:330
  24.8 3.5 %own_slots.1 = bf16[768,1280]{1,0:T(8,128)(2,1)} custom-call(bf16[128,128]{1,0:T(8,128)(2,1)S(1)} %codes.1.info_ref, bf16[128,1280]{1,0:T(8,128)(2,1)S(1)} %slice.33.x_ref), custom_call_target="tpu_custom_call" | custom-call | flops 251658240 | bytes 1966080 | tf_op jit(solution)/shard_map/own_slots/pallas_call | solution.py:188
  28.2 6.8 %all-to-all-start.1 = ((bf16[16,48,1280]{2,1,0:T(8,128)(2,1)}), bf16[16,48,1280]{2,1,0:T(8,128)(2,1)}, u32[]{:S(2)}, u32[]{:S(2)}) async-start(bf16[16,48,1280]{2,1,0:T(8,128)(2,1)} %bitcast.6), calls=%async_computation.1 | async-start | bytes 3932160 | tf_op jit(solution)/shard_map/all_to_all | solution.py:496
  36.5 3.5 %collective-permute-start.6 = (bf16[128,2432]{1,0:T(8,128)(2,1)}, bf16[128,2432]{1,0:T(8,128)(2,1)S(1)}, u32[]{:S(2)}, u32[]{:S(2)}) collective-permute-start(bf16[128,2432]{1,0:T(8,128)(2,1)} %collective-permute-done.5.refs_6_.refs_5_), channel_id=1, source_target_pairs={{0,14},{2,0},{4,2},{6,4},{8,6},{10,8},{12,10},{14,12},{1,15},{3,1}... | collective-permute-start | bytes 1867784 | tf_op jit(solution)/shard_map/ppermute | solution.py:330
  41.9 12.4 %collective-permute-done.3.refs_4_.refs_0_ = bf16[128,128]{1,0:T(8,128)(2,1)S(1)} collective-permute-done((bf16[128,128]{1,0:T(8,128)(2,1)S(1)}, bf16[128,128]{1,0:T(8,128)(2,1)S(1)}, u32[]{:S(2)}, u32[]{:S(2)}) %collective-permute-start.3) | collective-permute-done | bytes 32800 | tf_op jit(solution)/shard_map/ppermute | solution.py:492
  59.2 4.8 %collective-permute-start.17 = (bf16[1792,1024]{1,0:T(8,128)(2,1)}, bf16[1792,1024]{1,0:T(8,128)(2,1)}, u32[]{:S(2)}, u32[]{:S(2)}) collective-permute-start(bf16[1792,1024]{1,0:T(8,128)(2,1)} %bitcast.24), channel_id=1, source_target_pairs={{0,1},{1,0},{2,3},{3,2},{4,5},{5,4},{6,7},{7,6},{8,9},{9,8},{10,11... | collective-permute-start | bytes 11010056 | tf_op jit(solution)/shard_map/ppermute | solution.py:481
  64.1 3.3 %route.1 = (bf16[768,1024]{1,0:T(8,128)(2,1)S(1)}, bf16[768,128]{1,0:T(8,128)(2,1)S(1)}) custom-call(s32[1]{0:T(128)} %bitcast.3.z_ref, bf16[128,2432]{1,0:T(8,128)(2,1)S(1)} %pad_maximum_fusion.refs_0_, bf16[128,2432]{1,0:T(8,128)(2,1)S(1)} %collective-permute-done.refs_1_, bf16[128,2432]{1,0:T(8,128)(2,1)} %collective-permute-done.1.refs_2_, ...), custom_call_target="tpu_custom_call" | custom-call | flops 100000000 | bytes 2000000 | tf_op jit(solution)/shard_map/route/pallas_call | solution.py:91
  67.4 9.5 %pack.1 = bf16[768,2432]{1,0:T(8,128)(2,1)} custom-call(bf16[768,1024]{1,0:T(8,128)(2,1)S(1)} %get-tuple-element.19.select_ref, bf16[768,128]{1,0:T(8,128)(2,1)S(1)} %get-tuple-element.20.gate_ref, bf16[128,2432]{1,0:T(8,128)(2,1)S(1)} %pad_maximum_fusion.refs_0_, bf16[128,2432]{1,0:T(8,128)(2,1)S(1)} %collective-permute-done.refs_1_, ...), custom_call_target="tpu_custom_call" | custom-call | flops 3623878656 | bytes 9830400 | tf_op jit(solution)/shard_map/pack/pallas_call | solution.py:129
  76.9 6.8 %all-to-all-start = ((bf16[16,48,2432]{2,1,0:T(8,128)(2,1)}), bf16[16,48,2432]{2,1,0:T(8,128)(2,1)}, u32[]{:S(2)}, u32[]{:S(2)}) async-start(bf16[16,48,2432]{2,1,0:T(8,128)(2,1)} %bitcast.27), calls=%async_computation | async-start | bytes 7471104 | tf_op jit(solution)/shard_map/all_to_all | solution.py:503
  83.7 5.4 %turn.1 = (bf16[96,1280]{1,0:T(8,128)(2,1)S(1)}, bf16[96,1280]{1,0:T(8,128)(2,1)S(1)}, bf16[144,1280]{1,0:T(8,128)(2,1)S(1)}, bf16[96,1280]{1,0:T(8,128)(2,1)S(1...) custom-call(s32[1]{0:T(128)} %bitcast.3.z_ref, ...), custom_call_target="tpu_custom_call" | custom-call | flops 1509949440 | bytes 3932160 | tf_op jit(solution)/shard_map/turn/pallas_call | solution.py:236
  89.1 3.6 %collective-permute-start.13 = (bf16[144,1280]{1,0:T(8,128)(2,1)S(1)}, bf16[144,1280]{1,0:T(8,128)(2,1)S(1)}, u32[]{:S(2)}, u32[]{:S(2)}) collective-permute-start(bf16[144,1280]{1,0:T(8,128)(2,1)S(1)} %get-tuple-element.27), channel_id=1, source_target_pairs={{0,12},{2,14},{4,0},{6,2},{8,4},{10,6},{12,8},{14,10},{1,13},{3,15... | collective-permute-start | bytes 1105928 | tf_op jit(solution)/shard_map/ppermute | solution.py:256
  92.7 2.7 %collective-permute-start.11 = (bf16[96,1280]{1,0:T(8,128)(2,1)S(1)}, bf16[96,1280]{1,0:T(8,128)(2,1)S(1)}, u32[]{:S(2)}, u32[]{:S(2)}) collective-permute-start(bf16[96,1280]{1,0:T(8,128)(2,1)S(1)} %get-tuple-element.26), channel_id=1, source_target_pairs={{0,6},{2,8},{4,10},{6,12},{8,14},{10,0},{12,2},{14,4},{1,7},{3,9},... | collective-permute-start | bytes 737288 | tf_op jit(solution)/shard_map/ppermute | solution.py:256
  95.4 10.1 %collective-permute-done.10.refs_2_ = bf16[144,1280]{1,0:T(8,128)(2,1)S(1)} collective-permute-done((bf16[144,1280]{1,0:T(8,128)(2,1)S(1)}, bf16[144,1280]{1,0:T(8,128)(2,1)S(1)}, u32[]{:S(2)}, u32[]{:S(2)}) %collective-permute-start.10) | collective-permute-done | bytes 368672 | tf_op jit(solution)/shard_map/ppermute | solution.py:256
  110.5 5.3 %collective-permute-start.12 = (bf16[48,1280]{1,0:T(8,128)(2,1)S(1)}, bf16[48,1280]{1,0:T(8,128)(2,1)S(1)}, u32[]{:S(2)}, u32[]{:S(2)}) collective-permute-start(bf16[48,1280]{1,0:T(8,128)(2,1)S(1)} %slice.34), channel_id=1, source_target_pairs={{0,4},{2,6},{4,8},{6,10},{8,12},{10,14},{12,0},{14,2},{1,5},{3,7},... | collective-permute-start | bytes 368648 | tf_op jit(solution)/shard_map/ppermute | solution.py:256
  115.7 9.6 %collective-permute-done.11.refs_3_ = bf16[96,1280]{1,0:T(8,128)(2,1)S(1)} collective-permute-done((bf16[96,1280]{1,0:T(8,128)(2,1)S(1)}, bf16[96,1280]{1,0:T(8,128)(2,1)S(1)}, u32[]{:S(2)}, u32[]{:S(2)}) %collective-permute-start.11) | collective-permute-done | bytes 245792 | tf_op jit(solution)/shard_map/ppermute | solution.py:256
  125.4 4.0 %collective-permute-start.14 = (bf16[48,1280]{1,0:T(8,128)(2,1)S(1)}, bf16[48,1280]{1,0:T(8,128)(2,1)S(1)}, u32[]{:S(2)}, u32[]{:S(2)}) collective-permute-start(bf16[48,1280]{1,0:T(8,128)(2,1)S(1)} %slice.35), channel_id=1, source_target_pairs={{0,12},{2,14},{4,0},{6,2},{8,4},{10,6},{12,8},{14,10},{1,13},{3,15... | collective-permute-start | bytes 368648 | tf_op jit(solution)/shard_map/ppermute | solution.py:256
  129.3 5.6 %collective-permute-done.12.refs_4_ = bf16[48,1280]{1,0:T(8,128)(2,1)S(1)} collective-permute-done((bf16[48,1280]{1,0:T(8,128)(2,1)S(1)}, bf16[48,1280]{1,0:T(8,128)(2,1)S(1)}, u32[]{:S(2)}, u32[]{:S(2)}) %collective-permute-start.12) | collective-permute-done | bytes 122912 | tf_op jit(solution)/shard_map/ppermute | solution.py:256
  134.9 3.0 %settle.1.early_ref.y_ref = bf16[768,1280]{1,0:T(8,128)(2,1)S(1)} custom-call(s32[1]{0:T(128)} %bitcast.3.z_ref, bf16[96,1280]{1,0:T(8,128)(2,1)S(1)} %get-tuple-element.23.refs_0_, bf16[96,1280]{1,0:T(8,128)(2,1)S(1)} %collective-permute-done.9.refs_1_, bf16[144,1280]{1,0:T(8,128)(2,1)S(1)} %collective-permute-done.10.refs_2_, ...), custom_call_target="tpu_custom_call" | custom-call | flops 1509949440 | bytes 3932160 | tf_op jit(solution)/shard_map/settle/pallas_call | solution.py:279
  141.4 10.6 %back.1 = (bf16[768,1024]{1,0:T(8,128)(2,1)}, f32[128,128]{1,0:T(8,128)S(1)}, bf16[768,1024]{1,0:T(8,128)(2,1)S(1)}) custom-call(bf16[768,2432]{1,0:T(8,128)(2,1)} %bitcast.5.rows_ref.x_ref, bf16[768,1280]{1,0:T(8,128)(2,1)S(1)} %settle.1.early_ref.y_ref, bf16[768,1024]{1,0:T(8,128)(2,1)S(1)} %bitcast.26, ...), custom_call_target="tpu_custom_call" | custom-call | flops 5637144576 | bytes 18000000 | tf_op jit(solution)/shard_map/back/pallas_call | solution.py:371
  152.0 6.3 %convolution_convert_fusion = bf16[1792,1024]{1,0:T(8,128)(2,1)} fusion(bf16[768,1024]{1,0:T(8,128)(2,1)S(1)} %get-tuple-element.31.gated_ref, bf16[768,2432]{1,0:T(8,128)(2,1)} %bitcast.5.rows_ref.x_ref), kind=kOutput, calls=%fused_computation | convolution fusion | flops 2820407296 | bytes 7995392 | tf_op jit(solution)/shard_map/dot_general | solution.py:516
  159.9 13.7 %all-to-all-start.2 = ((f32[128,1,6]{2,1,0:T(1,128)}), f32[128,1,6]{2,1,0:T(1,128)}, u32[]{:S(2)}, u32[]{:S(2)}) async-start(f32[128,1,6]{2,1,0:T(1,128)} %bitcast.19), calls=%async_computation.2 | async-start | bytes 131072 | tf_op jit(solution)/shard_map/all_to_all | solution.py:509
  173.6 8.2 %down.1 = (bf16[1792,1024]{1,0:T(8,128)(2,1)}, f32[8,128]{1,0:T(8,128)S(1)}) custom-call(bf16[768,2432]{1,0:T(8,128)(2,1)} %bitcast.5.rows_ref.x_ref, bf16[768,1280]{1,0:T(8,128)(2,1)S(1)} %settle.1.early_ref.y_ref, bf16[768,1024]{1,0:T(8,128)(2,1)S(1)} %get-tuple-element.31.gated_ref, bf16[1792,1024]{1,0:T(8,128)(2,1)} %collective-permute-done.18.received_ref), custom_call_target="tpu_custom_call" | custom-call | flops 2818572288 | bytes 12000000 | tf_op jit(solution)/shard_map/down/pallas_call | solution.py:412
  (53 shorter events, 24.6 us)
Async XLA Ops:
  2.1 38.0 %copy-start = (bf16[128,128]{1,0:T(8,128)(2,1)}, bf16[128,128]{1,0:T(8,128)(2,1)S(1)}, u32[]{:S(2)}) copy-start(bf16[128,128]{1,0:T(8,128)(2,1)S(1)} %codes.1.info_ref) | copy-start | bytes 98308
  2.1 19.2 %collective-permute-start.4 = (bf16[128,2432]{1,0:T(8,128)(2,1)S(1)}, bf16[128,2432]{1,0:T(8,128)(2,1)S(1)}, u32[]{:S(2)}, u32[]{:S(2)}) collective-permute-start(bf16[128,2432]{1,0:T(8,128)(2,1)S(1)} %pad_maximum_fusion.refs_0_), channel_id=1, source_target_pairs={{0,14},{2,0},{4,2},{6,4},{8,6},{10,8},{12,10},{14,12},{1,15},{3,1}... | collective-permute-start | bytes 1867784 | tf_op jit(solution)/shard_map/ppermute | solution.py:330
  8.6 16.1 %collective-permute-start = (bf16[128,2432]{1,0:T(8,128)(2,1)S(1)}, bf16[128,2432]{1,0:T(8,128)(2,1)S(1)}, u32[]{:S(2)}, u32[]{:S(2)}) collective-permute-start(bf16[128,2432]{1,0:T(8,128)(2,1)S(1)} %pad_maximum_fusion.refs_0_), channel_id=1, source_target_pairs={{0,2},{2,4},{4,6},{6,8},{8,10},{10,12},{12,14},{14,0},{1,3},{3,5},... | collective-permute-start | bytes 1867784 | tf_op jit(solution)/shard_map/ppermute | solution.py:329
  21.3 15.2 %collective-permute-start.5 = (bf16[128,2432]{1,0:T(8,128)(2,1)S(1)}, bf16[128,2432]{1,0:T(8,128)(2,1)}, u32[]{:S(2)}, u32[]{:S(2)}) collective-permute-start(bf16[128,2432]{1,0:T(8,128)(2,1)S(1)} %collective-permute-done.4.refs_7_.refs_6_), channel_id=1, source_target_pairs={{0,14},{2,0},{4,2},{6,4},{8,6},{10,8},{12,10},{14,12},{1,15},{3,1}... | collective-permute-start | bytes 1867784 | tf_op jit(solution)/shard_map/ppermute | solution.py:330
  24.7 15.3 %collective-permute-start.1 = (bf16[128,2432]{1,0:T(8,128)(2,1)S(1)}, bf16[128,2432]{1,0:T(8,128)(2,1)}, u32[]{:S(2)}, u32[]{:S(2)}) collective-permute-start(bf16[128,2432]{1,0:T(8,128)(2,1)S(1)} %collective-permute-done.refs_1_), channel_id=1, source_target_pairs={{0,2},{2,4},{4,6},{6,8},{8,10},{10,12},{12,14},{14,0},{1,3},{3,5},... | collective-permute-start | bytes 1867784 | tf_op jit(solution)/shard_map/ppermute | solution.py:329
  28.2 48.7 %all-to-all-start.1 = ((bf16[16,48,1280]{2,1,0:T(8,128)(2,1)}), bf16[16,48,1280]{2,1,0:T(8,128)(2,1)}, u32[]{:S(2)}, u32[]{:S(2)}) async-start(bf16[16,48,1280]{2,1,0:T(8,128)(2,1)} %bitcast.6), calls=%async_computation.1 | async-start | bytes 3932160 | tf_op jit(solution)/shard_map/all_to_all | solution.py:496
  36.5 17.8 %collective-permute-start.6 = (bf16[128,2432]{1,0:T(8,128)(2,1)}, bf16[128,2432]{1,0:T(8,128)(2,1)S(1)}, u32[]{:S(2)}, u32[]{:S(2)}) collective-permute-start(bf16[128,2432]{1,0:T(8,128)(2,1)} %collective-permute-done.5.refs_6_.refs_5_), channel_id=1, source_target_pairs={{0,14},{2,0},{4,2},{6,4},{8,6},{10,8},{12,10},{14,12},{1,15},{3,1}... | collective-permute-start | bytes 1867784 | tf_op jit(solution)/shard_map/ppermute | solution.py:330
  40.0 15.0 %collective-permute-start.2 = (bf16[128,2432]{1,0:T(8,128)(2,1)}, bf16[128,2432]{1,0:T(8,128)(2,1)S(1)}, u32[]{:S(2)}, u32[]{:S(2)}) collective-permute-start(bf16[128,2432]{1,0:T(8,128)(2,1)} %collective-permute-done.1.refs_2_), channel_id=1, source_target_pairs={{0,2},{2,4},{4,6},{6,8},{8,10},{10,12},{12,14},{14,0},{1,3},{3,5},... | collective-permute-start | bytes 1867784 | tf_op jit(solution)/shard_map/ppermute | solution.py:329
  40.0 14.3 %collective-permute-start.3 = (bf16[128,128]{1,0:T(8,128)(2,1)S(1)}, bf16[128,128]{1,0:T(8,128)(2,1)S(1)}, u32[]{:S(2)}, u32[]{:S(2)}) collective-permute-start(bf16[128,128]{1,0:T(8,128)(2,1)S(1)} %codes.1.info_ref), channel_id=1, source_target_pairs={{0,8},{2,10},{4,12},{6,14},{8,0},{10,2},{12,4},{14,6},{1,9},{3,11}... | collective-permute-start | bytes 98312 | tf_op jit(solution)/shard_map/ppermute | solution.py:492
  56.6 10.8 %collective-permute-start.7 = (bf16[128,1152]{1,0:T(8,128)(2,1)}, bf16[128,1152]{1,0:T(8,128)(2,1)S(1)}, u32[]{:S(2)}, u32[]{:S(2)}) collective-permute-start(bf16[128,1152]{1,0:T(8,128)(2,1)} %get-tuple-element.21), channel_id=1, source_target_pairs={{0,2},{2,4},{4,6},{6,8},{8,10},{10,12},{12,14},{14,0},{1,3},{3,5},... | collective-permute-start | bytes 884744 | tf_op jit(solution)/shard_map/ppermute | solution.py:339
  56.6 10.8 %collective-permute-start.8 = (bf16[128,1152]{1,0:T(8,128)(2,1)}, bf16[128,1152]{1,0:T(8,128)(2,1)}, u32[]{:S(2)}, u32[]{:S(2)}) collective-permute-start(bf16[128,1152]{1,0:T(8,128)(2,1)} %get-tuple-element.22), channel_id=1, source_target_pairs={{0,14},{2,0},{4,2},{6,4},{8,6},{10,8},{12,10},{14,12},{1,15},{3,1}... | collective-permute-start | bytes 884744 | tf_op jit(solution)/shard_map/ppermute | solution.py:339
  59.2 78.7 %collective-permute-start.17 = (bf16[1792,1024]{1,0:T(8,128)(2,1)}, bf16[1792,1024]{1,0:T(8,128)(2,1)}, u32[]{:S(2)}, u32[]{:S(2)}) collective-permute-start(bf16[1792,1024]{1,0:T(8,128)(2,1)} %bitcast.24), channel_id=1, source_target_pairs={{0,1},{1,0},{2,3},{3,2},{4,5},{5,4},{6,7},{7,6},{8,9},{9,8},{10,11... | collective-permute-start | bytes 11010056 | tf_op jit(solution)/shard_map/ppermute | solution.py:481
  76.9 61.1 %all-to-all-start = ((bf16[16,48,2432]{2,1,0:T(8,128)(2,1)}), bf16[16,48,2432]{2,1,0:T(8,128)(2,1)}, u32[]{:S(2)}, u32[]{:S(2)}) async-start(bf16[16,48,2432]{2,1,0:T(8,128)(2,1)} %bitcast.27), calls=%async_computation | async-start | bytes 7471104 | tf_op jit(solution)/shard_map/all_to_all | solution.py:503
  89.0 16.5 %collective-permute-start.10 = (bf16[144,1280]{1,0:T(8,128)(2,1)S(1)}, bf16[144,1280]{1,0:T(8,128)(2,1)S(1)}, u32[]{:S(2)}, u32[]{:S(2)}) collective-permute-start(bf16[144,1280]{1,0:T(8,128)(2,1)S(1)} %get-tuple-element.25), channel_id=1, source_target_pairs={{0,4},{2,6},{4,8},{6,10},{8,12},{10,14},{12,0},{14,2},{1,5},{3,7},... | collective-permute-start | bytes 1105928 | tf_op jit(solution)/shard_map/ppermute | solution.py:256
  89.1 16.6 %collective-permute-start.13 = (bf16[144,1280]{1,0:T(8,128)(2,1)S(1)}, bf16[144,1280]{1,0:T(8,128)(2,1)S(1)}, u32[]{:S(2)}, u32[]{:S(2)}) collective-permute-start(bf16[144,1280]{1,0:T(8,128)(2,1)S(1)} %get-tuple-element.27), channel_id=1, source_target_pairs={{0,12},{2,14},{4,0},{6,2},{8,4},{10,6},{12,8},{14,10},{1,13},{3,15... | collective-permute-start | bytes 1105928 | tf_op jit(solution)/shard_map/ppermute | solution.py:256
  92.7 17.8 %collective-permute-start.9 = (bf16[96,1280]{1,0:T(8,128)(2,1)S(1)}, bf16[96,1280]{1,0:T(8,128)(2,1)S(1)}, u32[]{:S(2)}, u32[]{:S(2)}) collective-permute-start(bf16[96,1280]{1,0:T(8,128)(2,1)S(1)} %get-tuple-element.24), channel_id=1, source_target_pairs={{0,2},{2,4},{4,6},{6,8},{8,10},{10,12},{12,14},{14,0},{1,3},{3,5},... | collective-permute-start | bytes 737288 | tf_op jit(solution)/shard_map/ppermute | solution.py:256
  92.7 32.7 %collective-permute-start.11 = (bf16[96,1280]{1,0:T(8,128)(2,1)S(1)}, bf16[96,1280]{1,0:T(8,128)(2,1)S(1)}, u32[]{:S(2)}, u32[]{:S(2)}) collective-permute-start(bf16[96,1280]{1,0:T(8,128)(2,1)S(1)} %get-tuple-element.26), channel_id=1, source_target_pairs={{0,6},{2,8},{4,10},{6,12},{8,14},{10,0},{12,2},{14,4},{1,7},{3,9},... | collective-permute-start | bytes 737288 | tf_op jit(solution)/shard_map/ppermute | solution.py:256
  105.5 23.8 %collective-permute-start.15 = (bf16[96,1280]{1,0:T(8,128)(2,1)S(1)}, bf16[96,1280]{1,0:T(8,128)(2,1)S(1)}, u32[]{:S(2)}, u32[]{:S(2)}) collective-permute-start(bf16[96,1280]{1,0:T(8,128)(2,1)S(1)} %get-tuple-element.28), channel_id=1, source_target_pairs={{0,10},{2,12},{4,14},{6,0},{8,2},{10,4},{12,6},{14,8},{1,11},{3,13... | collective-permute-start | bytes 737288 | tf_op jit(solution)/shard_map/ppermute | solution.py:256
  105.8 23.6 %collective-permute-start.16 = (bf16[96,1280]{1,0:T(8,128)(2,1)S(1)}, bf16[96,1280]{1,0:T(8,128)(2,1)S(1)}, u32[]{:S(2)}, u32[]{:S(2)}) collective-permute-start(bf16[96,1280]{1,0:T(8,128)(2,1)S(1)} %get-tuple-element.29), channel_id=1, source_target_pairs={{0,14},{2,0},{4,2},{6,4},{8,6},{10,8},{12,10},{14,12},{1,15},{3,1}... | collective-permute-start | bytes 737288 | tf_op jit(solution)/shard_map/ppermute | solution.py:256
  110.5 24.4 %collective-permute-start.12 = (bf16[48,1280]{1,0:T(8,128)(2,1)S(1)}, bf16[48,1280]{1,0:T(8,128)(2,1)S(1)}, u32[]{:S(2)}, u32[]{:S(2)}) collective-permute-start(bf16[48,1280]{1,0:T(8,128)(2,1)S(1)} %slice.34), channel_id=1, source_target_pairs={{0,4},{2,6},{4,8},{6,10},{8,12},{10,14},{12,0},{14,2},{1,5},{3,7},... | collective-permute-start | bytes 368648 | tf_op jit(solution)/shard_map/ppermute | solution.py:256
  125.4 9.6 %collective-permute-start.14 = (bf16[48,1280]{1,0:T(8,128)(2,1)S(1)}, bf16[48,1280]{1,0:T(8,128)(2,1)S(1)}, u32[]{:S(2)}, u32[]{:S(2)}) collective-permute-start(bf16[48,1280]{1,0:T(8,128)(2,1)S(1)} %slice.35), channel_id=1, source_target_pairs={{0,12},{2,14},{4,0},{6,2},{8,4},{10,6},{12,8},{14,10},{1,13},{3,15... | collective-permute-start | bytes 368648 | tf_op jit(solution)/shard_map/ppermute | solution.py:256
  152.0 6.3 %copy-start.2 = (f32[128,128]{1,0:T(8,128)}, f32[128,128]{1,0:T(8,128)S(1)}, u32[]{:S(2)}) copy-start(f32[128,128]{1,0:T(8,128)S(1)} %get-tuple-element.30) | copy-start | bytes 196612
  158.3 15.3 %collective-permute-start.18 = (bf16[1792,1024]{1,0:T(8,128)(2,1)}, bf16[1792,1024]{1,0:T(8,128)(2,1)}, u32[]{:S(2)}, u32[]{:S(2)}) collective-permute-start(bf16[1792,1024]{1,0:T(8,128)(2,1)} %convolution_convert_fusion), channel_id=1, source_target_pairs={{0,1},{1,0},{2,3},{3,2},{4,5},{5,4},{6,7},{7,6},{8,9},{9,8},{10,11... | collective-permute-start | bytes 11010056 | tf_op jit(solution)/shard_map/ppermute | solution.py:519
  159.9 24.3 %all-to-all-start.2 = ((f32[128,1,6]{2,1,0:T(1,128)}), f32[128,1,6]{2,1,0:T(1,128)}, u32[]{:S(2)}, u32[]{:S(2)}) async-start(f32[128,1,6]{2,1,0:T(1,128)} %bitcast.19), calls=%async_computation.2 | async-start | bytes 131072 | tf_op jit(solution)/shard_map/all_to_all | solution.py:509
  (6 other events, 8.1 us)

commit v4 on v3

--- a/solution.py
+++ b/solution.py
@@ -10,7 +10,7 @@
 route_scale = 2.5
 bf16 = jnp.bfloat16
 f32 = jnp.float32
-EARLY = 1280
+EARLY = 1024
 NODES = 16
 RING = 8
 CAP = 6
@@ -18,7 +18,7 @@
 BLOCK = RING * CAP
 LANES = 128
 SLOTS = NODES * BLOCK
-RING_SPLIT = 1152
+RING_SPLIT = 1280
 VMEM_LIMIT = 14 * 2**20
 
 
@@ -121,7 +121,7 @@
 
 
 def pack(select, gate_column, pieces, first, second):
-    tile = 384
+    tile = 640
     halfway = RING_SPLIT // tile
     width = 2 * RING_SPLIT
     near = pl.BlockSpec((LANES, tile), lambda i: (0, jnp.minimum(i, 2 * halfway - 1)))
@@ -301,7 +301,7 @@
 
 
 def halves(up, down, later):
-    tile = 384
+    tile = 256
     steps = RING_SPLIT // tile
     line = lambda i: (0, i)
     return pl.pallas_call(

time: 187 us -> 187 us (level)
  waiting for transfers between devices: 57.8 us -> 63.3 us
  starting transfers between devices: 69.3 us -> 64.3 us
  Pallas kernels: 46.8 us -> 43.1 us
  local copies, waits for them, and re-layouts: 4.27 us -> 7.38 us
    ppermute x8, starting transfers between devices: 17.7 us -> 11.8 us  [step(): return lax.ppermute(x, 'local', [(i, (i + k) % RING) for i in range(RING)])]
    ppermute x3, waiting for transfers between devices: 14.2 us -> 17.7 us  [ring(): down = lax.ppermute(down, 'local', back)]
    unnamed x16 -> x14, local copies, waits for them, and re-layouts: 4.22 us -> 7.33 us
  transfers between devices with their start and end apart: 22 -> 22, of which waited for: 10 -> 12; matrix products, arithmetic and copies ran while one was open for 0% -> 0% of each run, Pallas kernels for 18% -> 17%
where the time goes in v4:
time: 187 us; the launch traced here: 186 us
  starting transfers between devices  64.3 us (34%)
  waiting for transfers between devices  63.3 us (34%)
  Pallas kernels  43.1 us (23%)
  local copies, waits for them, and re-layouts  7.38 us (4%)
  matrix products  6.28 us (3%)
    ppermute x8, waiting for transfers between devices, step(): return lax.ppermute(x, 'local', [(i, (i + k) % RING) for i in range(RING)])  27.4 us
    ppermute x3, waiting for transfers between devices, ring(): down = lax.ppermute(down, 'local', back)  17.7 us
    ppermute x1, waiting for transfers between devices, local(): lax.ppermute(info, 'local', [(i, (i + middle) % RING) for i in range(RING)])  14.2 us
    ppermute x3, starting transfers between devices, ring(): down = lax.ppermute(down, 'local', back)  13.4 us
    all_to_all x1, starting transfers between devices, local(): lax.all_to_all(gate_grad[:, :CAP], ('node', 'local'), split_axis=0, conca...  13.3 us
    ppermute x8, starting transfers between devices, step(): return lax.ppermute(x, 'local', [(i, (i + k) % RING) for i in range(RING)])  11.8 us
    pallas_call x1, Pallas kernels, back(): pl.pallas_call(functools.partial(back_kernel, half - early.shape[1]), gri...  9.64 us
    pallas_call x1, Pallas kernels, pack(): pl.pallas_call(functools.partial(pack_kernel, halfway), grid=(2 * halfway...  8.86 us
  transfers between devices with their start and end apart: 22, of which 12 were waited for; matrix products, arithmetic and copies ran while one was open for 0% of the time, Pallas kernels for 17%

profile of v4, /device:TPU:1, one launch (start us, length us, event | category | flops | bytes accessed | tf_op | source)
XLA Modules:
  0.0 186.5 jit_solution(9885222707589187330)
XLA Ops:
  2.1 6.5 %collective-permute-start.4 = (bf16[128,2688]{1,0:T(8,128)(2,1)S(1)}, bf16[128,2688]{1,0:T(8,128)(2,1)S(1)}, u32[]{:S(2)}, u32[]{:S(2)}) collective-permute-start(bf16[128,2688]{1,0:T(8,128)(2,1)S(1)} %pad_maximum_fusion.refs_0_), channel_id=1, source_target_pairs={{0,14},{2,0},{4,2},{6,4},{8,6},{10,8},{12,10},{14,12},{1,15},{3,1}... | collective-permute-start | bytes 2064392 | tf_op jit(solution)/shard_map/ppermute | solution.py:330
  8.6 14.1 %collective-permute-done.4.refs_7_.refs_6_ = bf16[128,2688]{1,0:T(8,128)(2,1)S(1)} collective-permute-done((bf16[128,2688]{1,0:T(8,128)(2,1)S(1)}, bf16[128,2688]{1,0:T(8,128)(2,1)S(1)}, u32[]{:S(2)}, u32[]{:S(2)}) %collective-permute-start.4) | collective-permute-done | bytes 688160 | tf_op jit(solution)/shard_map/ppermute | solution.py:330
  22.7 3.4 %collective-permute-start.5 = (bf16[128,2688]{1,0:T(8,128)(2,1)S(1)}, bf16[128,2688]{1,0:T(8,128)(2,1)}, u32[]{:S(2)}, u32[]{:S(2)}) collective-permute-start(bf16[128,2688]{1,0:T(8,128)(2,1)S(1)} %collective-permute-done.4.refs_7_.refs_6_), channel_id=1, source_target_pairs={{0,14},{2,0},{4,2},{6,4},{8,6},{10,8},{12,10},{14,12},{1,15},{3,1}... | collective-permute-start | bytes 2064392 | tf_op jit(solution)/shard_map/ppermute | solution.py:330
  26.2 2.7 %own_slots.1 = bf16[768,1024]{1,0:T(8,128)(2,1)} custom-call(bf16[128,128]{1,0:T(8,128)(2,1)S(1)} %codes.1.info_ref, bf16[128,1024]{1,0:T(8,128)(2,1)S(1)} %slice.33.x_ref), custom_call_target="tpu_custom_call" | custom-call | flops 201326592 | bytes 1572864 | tf_op jit(solution)/shard_map/own_slots/pallas_call | solution.py:188
  28.9 6.8 %all-to-all-start.1 = ((bf16[16,48,1024]{2,1,0:T(8,128)(2,1)}), bf16[16,48,1024]{2,1,0:T(8,128)(2,1)}, u32[]{:S(2)}, u32[]{:S(2)}) async-start(bf16[16,48,1024]{2,1,0:T(8,128)(2,1)} %bitcast.6), calls=%async_computation.1 | async-start | bytes 3145728 | tf_op jit(solution)/shard_map/all_to_all | solution.py:496
  35.7 3.6 %collective-permute-done.5.refs_6_.refs_5_ = bf16[128,2688]{1,0:T(8,128)(2,1)} collective-permute-done((bf16[128,2688]{1,0:T(8,128)(2,1)S(1)}, bf16[128,2688]{1,0:T(8,128)(2,1)}, u32[]{:S(2)}, u32[]{:S(2)}) %collective-permute-start.5) | collective-permute-done | bytes 688160 | tf_op jit(solution)/shard_map/ppermute | solution.py:330
  39.3 3.5 %collective-permute-start.6 = (bf16[128,2688]{1,0:T(8,128)(2,1)}, bf16[128,2688]{1,0:T(8,128)(2,1)S(1)}, u32[]{:S(2)}, u32[]{:S(2)}) collective-permute-start(bf16[128,2688]{1,0:T(8,128)(2,1)} %collective-permute-done.5.refs_6_.refs_5_), channel_id=1, source_target_pairs={{0,14},{2,0},{4,2},{6,4},{8,6},{10,8},{12,10},{14,12},{1,15},{3,1}... | collective-permute-start | bytes 2064392 | tf_op jit(solution)/shard_map/ppermute | solution.py:330
  44.6 14.2 %collective-permute-done.3.refs_4_.refs_0_ = bf16[128,128]{1,0:T(8,128)(2,1)S(1)} collective-permute-done((bf16[128,128]{1,0:T(8,128)(2,1)S(1)}, bf16[128,128]{1,0:T(8,128)(2,1)S(1)}, u32[]{:S(2)}, u32[]{:S(2)}) %collective-permute-start.3) | collective-permute-done | bytes 32800 | tf_op jit(solution)/shard_map/ppermute | solution.py:492
  61.3 2.7 %collective-permute-start.8 = (bf16[128,1280]{1,0:T(8,128)(2,1)}, bf16[128,1280]{1,0:T(8,128)(2,1)}, u32[]{:S(2)}, u32[]{:S(2)}) collective-permute-start(bf16[128,1280]{1,0:T(8,128)(2,1)} %get-tuple-element.22), channel_id=1, source_target_pairs={{0,14},{2,0},{4,2},{6,4},{8,6},{10,8},{12,10},{14,12},{1,15},{3,1}... | collective-permute-start | bytes 983048 | tf_op jit(solution)/shard_map/ppermute | solution.py:339
  63.9 3.3 %route.1 = (bf16[768,1024]{1,0:T(8,128)(2,1)S(1)}, bf16[768,128]{1,0:T(8,128)(2,1)S(1)}) custom-call(s32[1]{0:T(128)} %bitcast.3.z_ref, bf16[128,2688]{1,0:T(8,128)(2,1)S(1)} %pad_maximum_fusion.refs_0_, bf16[128,2688]{1,0:T(8,128)(2,1)S(1)} %collective-permute-done.refs_1_, bf16[128,2688]{1,0:T(8,128)(2,1)} %collective-permute-done.1.refs_2_, ...), custom_call_target="tpu_custom_call" | custom-call | flops 100000000 | bytes 2000000 | tf_op jit(solution)/shard_map/route/pallas_call | solution.py:91
  68.7 8.9 %pack.1 = bf16[768,2688]{1,0:T(8,128)(2,1)} custom-call(bf16[768,1024]{1,0:T(8,128)(2,1)S(1)} %get-tuple-element.19.select_ref, bf16[768,128]{1,0:T(8,128)(2,1)S(1)} %get-tuple-element.20.gate_ref, bf16[128,2688]{1,0:T(8,128)(2,1)S(1)} %pad_maximum_fusion.refs_0_, bf16[128,2688]{1,0:T(8,128)(2,1)S(1)} %collective-permute-done.refs_1_, ...), custom_call_target="tpu_custom_call" | custom-call | flops 4026531840 | bytes 10747904 | tf_op jit(solution)/shard_map/pack/pallas_call | solution.py:129
  77.6 6.8 %all-to-all-start = ((bf16[16,48,2688]{2,1,0:T(8,128)(2,1)}), bf16[16,48,2688]{2,1,0:T(8,128)(2,1)}, u32[]{:S(2)}, u32[]{:S(2)}) async-start(bf16[16,48,2688]{2,1,0:T(8,128)(2,1)} %bitcast.27), calls=%async_computation | async-start | bytes 8257536 | tf_op jit(solution)/shard_map/all_to_all | solution.py:503
  84.4 6.1 %collective-permute-start.17 = (bf16[1792,1024]{1,0:T(8,128)(2,1)}, bf16[1792,1024]{1,0:T(8,128)(2,1)S(1)}, u32[]{:S(2)}, u32[]{:S(2)}) collective-permute-start(bf16[1792,1024]{1,0:T(8,128)(2,1)} %bitcast.24), channel_id=1, source_target_pairs={{0,1},{1,0},{2,3},{3,2},{4,5},{5,4},{6,7},{7,6},{8,9},{9,8},{10,11... | collective-permute-start | bytes 11010056 | tf_op jit(solution)/shard_map/ppermute | solution.py:481
  90.4 4.4 %turn.1 = (bf16[96,1024]{1,0:T(8,128)(2,1)S(1)}, bf16[96,1024]{1,0:T(8,128)(2,1)S(1)}, bf16[144,1024]{1,0:T(8,128)(2,1)S(1)}, bf16[96,1024]{1,0:T(8,128)(2,1)S(1...) custom-call(s32[1]{0:T(128)} %bitcast.3.z_ref, ...), custom_call_target="tpu_custom_call" | custom-call | flops 1207959552 | bytes 3145728 | tf_op jit(solution)/shard_map/turn/pallas_call | solution.py:236
  95.2 3.3 %collective-permute-start.13 = (bf16[144,1024]{1,0:T(8,128)(2,1)S(1)}, bf16[144,1024]{1,0:T(8,128)(2,1)S(1)}, u32[]{:S(2)}, u32[]{:S(2)}) collective-permute-start(bf16[144,1024]{1,0:T(8,128)(2,1)S(1)} %get-tuple-element.27), channel_id=1, source_target_pairs={{0,12},{2,14},{4,0},{6,2},{8,4},{10,6},{12,8},{14,10},{1,13},{3,15... | collective-permute-start | bytes 884744 | tf_op jit(solution)/shard_map/ppermute | solution.py:256
  101.2 7.5 %collective-permute-done.10.refs_2_ = bf16[144,1024]{1,0:T(8,128)(2,1)S(1)} collective-permute-done((bf16[144,1024]{1,0:T(8,128)(2,1)S(1)}, bf16[144,1024]{1,0:T(8,128)(2,1)S(1)}, u32[]{:S(2)}, u32[]{:S(2)}) %collective-permute-start.10) | collective-permute-done | bytes 294944 | tf_op jit(solution)/shard_map/ppermute | solution.py:256
  108.7 4.9 %collective-permute-start.15 = (bf16[96,1024]{1,0:T(8,128)(2,1)S(1)}, bf16[96,1024]{1,0:T(8,128)(2,1)S(1)}, u32[]{:S(2)}, u32[]{:S(2)}) collective-permute-start(bf16[96,1024]{1,0:T(8,128)(2,1)S(1)} %get-tuple-element.28), channel_id=1, source_target_pairs={{0,10},{2,12},{4,14},{6,0},{8,2},{10,4},{12,6},{14,8},{1,11},{3,13... | collective-permute-start | bytes 589832 | tf_op jit(solution)/shard_map/ppermute | solution.py:256
  116.0 13.3 %collective-permute-done.11.refs_3_ = bf16[96,1024]{1,0:T(8,128)(2,1)S(1)} collective-permute-done((bf16[96,1024]{1,0:T(8,128)(2,1)S(1)}, bf16[96,1024]{1,0:T(8,128)(2,1)S(1)}, u32[]{:S(2)}, u32[]{:S(2)}) %collective-permute-start.11) | collective-permute-done | bytes 196640 | tf_op jit(solution)/shard_map/ppermute | solution.py:256
  131.7 2.4 %collective-permute-done.14.refs_5_ = bf16[48,1024]{1,0:T(8,128)(2,1)S(1)} collective-permute-done((bf16[48,1024]{1,0:T(8,128)(2,1)S(1)}, bf16[48,1024]{1,0:T(8,128)(2,1)S(1)}, u32[]{:S(2)}, u32[]{:S(2)}) %collective-permute-start.14) | collective-permute-done | bytes 98336 | tf_op jit(solution)/shard_map/ppermute | solution.py:256
  134.1 2.6 %settle.1.early_ref.y_ref = bf16[768,1024]{1,0:T(8,128)(2,1)S(1)} custom-call(s32[1]{0:T(128)} %bitcast.3.z_ref, bf16[96,1024]{1,0:T(8,128)(2,1)S(1)} %get-tuple-element.23.refs_0_, bf16[96,1024]{1,0:T(8,128)(2,1)S(1)} %collective-permute-done.9.refs_1_, bf16[144,1024]{1,0:T(8,128)(2,1)S(1)} %collective-permute-done.10.refs_2_, ...), custom_call_target="tpu_custom_call" | custom-call | flops 1207959552 | bytes 3145728 | tf_op jit(solution)/shard_map/settle/pallas_call | solution.py:279
  144.0 9.6 %back.1 = (bf16[768,1024]{1,0:T(8,128)(2,1)}, f32[128,128]{1,0:T(8,128)}, bf16[768,1024]{1,0:T(8,128)(2,1)S(1)}) custom-call(bf16[768,2688]{1,0:T(8,128)(2,1)} %bitcast.5.rows_ref.x_ref, bf16[768,1024]{1,0:T(8,128)(2,1)S(1)} %settle.1.early_ref.y_ref, bf16[768,1024]{1,0:T(8,128)(2,1)S(1)} %bitcast.26, bf16[1792,1024]{1,0:T(8,128)(2,1)S(1)} %copy-done.5, ...), custom_call_target="tpu_custom_call" | custom-call | flops 5637144576 | bytes 18000000 | tf_op jit(solution)/shard_map/back/pallas_call | solution.py:371
  153.7 6.3 %convolution_convert_fusion = bf16[1792,1024]{1,0:T(8,128)(2,1)} fusion(bf16[768,1024]{1,0:T(8,128)(2,1)S(1)} %get-tuple-element.31.gated_ref, bf16[768,2688]{1,0:T(8,128)(2,1)} %bitcast.5.rows_ref.x_ref), kind=kOutput, calls=%fused_computation | convolution fusion | flops 2820407296 | bytes 7995392 | tf_op jit(solution)/shard_map/dot_general | solution.py:516
  161.7 13.3 %all-to-all-start.2 = ((f32[128,1,6]{2,1,0:T(1,128)}), f32[128,1,6]{2,1,0:T(1,128)S(1)}, u32[]{:S(2)}, u32[]{:S(2)}) async-start(f32[128,1,6]{2,1,0:T(1,128)} %bitcast.11), calls=%async_computation.2 | async-start | bytes 131072 | tf_op jit(solution)/shard_map/all_to_all | solution.py:509
  175.0 8.4 %down.1 = (bf16[1792,1024]{1,0:T(8,128)(2,1)}, f32[8,128]{1,0:T(8,128)S(1)}) custom-call(bf16[768,2688]{1,0:T(8,128)(2,1)} %bitcast.5.rows_ref.x_ref, bf16[768,1024]{1,0:T(8,128)(2,1)S(1)} %settle.1.early_ref.y_ref, bf16[768,1024]{1,0:T(8,128)(2,1)S(1)} %get-tuple-element.31.gated_ref, bf16[1792,1024]{1,0:T(8,128)(2,1)} %collective-permute-done.18.received_ref), custom_call_target="tpu_custom_call" | custom-call | flops 2818572288 | bytes 12000000 | tf_op jit(solution)/shard_map/down/pallas_call | solution.py:412
  (51 shorter events, 27.1 us)
Async XLA Ops:
  2.1 20.6 %collective-permute-start.4 = (bf16[128,2688]{1,0:T(8,128)(2,1)S(1)}, bf16[128,2688]{1,0:T(8,128)(2,1)S(1)}, u32[]{:S(2)}, u32[]{:S(2)}) collective-permute-start(bf16[128,2688]{1,0:T(8,128)(2,1)S(1)} %pad_maximum_fusion.refs_0_), channel_id=1, source_target_pairs={{0,14},{2,0},{4,2},{6,4},{8,6},{10,8},{12,10},{14,12},{1,15},{3,1}... | collective-permute-start | bytes 2064392 | tf_op jit(solution)/shard_map/ppermute | solution.py:330
  8.6 17.5 %collective-permute-start = (bf16[128,2688]{1,0:T(8,128)(2,1)S(1)}, bf16[128,2688]{1,0:T(8,128)(2,1)S(1)}, u32[]{:S(2)}, u32[]{:S(2)}) collective-permute-start(bf16[128,2688]{1,0:T(8,128)(2,1)S(1)} %pad_maximum_fusion.refs_0_), channel_id=1, source_target_pairs={{0,2},{2,4},{4,6},{6,8},{8,10},{10,12},{12,14},{14,0},{1,3},{3,5},... | collective-permute-start | bytes 2064392 | tf_op jit(solution)/shard_map/ppermute | solution.py:329
  22.7 16.6 %collective-permute-start.5 = (bf16[128,2688]{1,0:T(8,128)(2,1)S(1)}, bf16[128,2688]{1,0:T(8,128)(2,1)}, u32[]{:S(2)}, u32[]{:S(2)}) collective-permute-start(bf16[128,2688]{1,0:T(8,128)(2,1)S(1)} %collective-permute-done.4.refs_7_.refs_6_), channel_id=1, source_target_pairs={{0,14},{2,0},{4,2},{6,4},{8,6},{10,8},{12,10},{14,12},{1,15},{3,1}... | collective-permute-start | bytes 2064392 | tf_op jit(solution)/shard_map/ppermute | solution.py:330
  26.1 16.7 %collective-permute-start.1 = (bf16[128,2688]{1,0:T(8,128)(2,1)S(1)}, bf16[128,2688]{1,0:T(8,128)(2,1)}, u32[]{:S(2)}, u32[]{:S(2)}) collective-permute-start(bf16[128,2688]{1,0:T(8,128)(2,1)S(1)} %collective-permute-done.refs_1_), channel_id=1, source_target_pairs={{0,2},{2,4},{4,6},{6,8},{8,10},{10,12},{12,14},{14,0},{1,3},{3,5},... | collective-permute-start | bytes 2064392 | tf_op jit(solution)/shard_map/ppermute | solution.py:329
  28.9 48.7 %all-to-all-start.1 = ((bf16[16,48,1024]{2,1,0:T(8,128)(2,1)}), bf16[16,48,1024]{2,1,0:T(8,128)(2,1)}, u32[]{:S(2)}, u32[]{:S(2)}) async-start(bf16[16,48,1024]{2,1,0:T(8,128)(2,1)} %bitcast.6), calls=%async_computation.1 | async-start | bytes 3145728 | tf_op jit(solution)/shard_map/all_to_all | solution.py:496
  39.3 19.5 %collective-permute-start.6 = (bf16[128,2688]{1,0:T(8,128)(2,1)}, bf16[128,2688]{1,0:T(8,128)(2,1)S(1)}, u32[]{:S(2)}, u32[]{:S(2)}) collective-permute-start(bf16[128,2688]{1,0:T(8,128)(2,1)} %collective-permute-done.5.refs_6_.refs_5_), channel_id=1, source_target_pairs={{0,14},{2,0},{4,2},{6,4},{8,6},{10,8},{12,10},{14,12},{1,15},{3,1}... | collective-permute-start | bytes 2064392 | tf_op jit(solution)/shard_map/ppermute | solution.py:330
  42.8 16.3 %collective-permute-start.2 = (bf16[128,2688]{1,0:T(8,128)(2,1)}, bf16[128,2688]{1,0:T(8,128)(2,1)S(1)}, u32[]{:S(2)}, u32[]{:S(2)}) collective-permute-start(bf16[128,2688]{1,0:T(8,128)(2,1)} %collective-permute-done.1.refs_2_), channel_id=1, source_target_pairs={{0,2},{2,4},{4,6},{6,8},{8,10},{10,12},{12,14},{14,0},{1,3},{3,5},... | collective-permute-start | bytes 2064392 | tf_op jit(solution)/shard_map/ppermute | solution.py:329
  42.8 16.0 %collective-permute-start.3 = (bf16[128,128]{1,0:T(8,128)(2,1)S(1)}, bf16[128,128]{1,0:T(8,128)(2,1)S(1)}, u32[]{:S(2)}, u32[]{:S(2)}) collective-permute-start(bf16[128,128]{1,0:T(8,128)(2,1)S(1)} %codes.1.info_ref), channel_id=1, source_target_pairs={{0,8},{2,10},{4,12},{6,14},{8,0},{10,2},{12,4},{14,6},{1,9},{3,11}... | collective-permute-start | bytes 98312 | tf_op jit(solution)/shard_map/ppermute | solution.py:492
  61.3 7.5 %collective-permute-start.7 = (bf16[128,1280]{1,0:T(8,128)(2,1)}, bf16[128,1280]{1,0:T(8,128)(2,1)}, u32[]{:S(2)}, u32[]{:S(2)}) collective-permute-start(bf16[128,1280]{1,0:T(8,128)(2,1)} %get-tuple-element.21), channel_id=1, source_target_pairs={{0,2},{2,4},{4,6},{6,8},{8,10},{10,12},{12,14},{14,0},{1,3},{3,5},... | collective-permute-start | bytes 983048 | tf_op jit(solution)/shard_map/ppermute | solution.py:339
  61.3 7.5 %collective-permute-start.8 = (bf16[128,1280]{1,0:T(8,128)(2,1)}, bf16[128,1280]{1,0:T(8,128)(2,1)}, u32[]{:S(2)}, u32[]{:S(2)}) collective-permute-start(bf16[128,1280]{1,0:T(8,128)(2,1)} %get-tuple-element.22), channel_id=1, source_target_pairs={{0,14},{2,0},{4,2},{6,4},{8,6},{10,8},{12,10},{14,12},{1,15},{3,1}... | collective-permute-start | bytes 983048 | tf_op jit(solution)/shard_map/ppermute | solution.py:339
  77.6 61.0 %all-to-all-start = ((bf16[16,48,2688]{2,1,0:T(8,128)(2,1)}), bf16[16,48,2688]{2,1,0:T(8,128)(2,1)}, u32[]{:S(2)}, u32[]{:S(2)}) async-start(bf16[16,48,2688]{2,1,0:T(8,128)(2,1)} %bitcast.27), calls=%async_computation | async-start | bytes 8257536 | tf_op jit(solution)/shard_map/all_to_all | solution.py:503
  84.4 52.3 %collective-permute-start.17 = (bf16[1792,1024]{1,0:T(8,128)(2,1)}, bf16[1792,1024]{1,0:T(8,128)(2,1)S(1)}, u32[]{:S(2)}, u32[]{:S(2)}) collective-permute-start(bf16[1792,1024]{1,0:T(8,128)(2,1)} %bitcast.24), channel_id=1, source_target_pairs={{0,1},{1,0},{2,3},{3,2},{4,5},{5,4},{6,7},{7,6},{8,9},{9,8},{10,11... | collective-permute-start | bytes 11010056 | tf_op jit(solution)/shard_map/ppermute | solution.py:481
  94.9 13.9 %collective-permute-start.10 = (bf16[144,1024]{1,0:T(8,128)(2,1)S(1)}, bf16[144,1024]{1,0:T(8,128)(2,1)S(1)}, u32[]{:S(2)}, u32[]{:S(2)}) collective-permute-start(bf16[144,1024]{1,0:T(8,128)(2,1)S(1)} %get-tuple-element.25), channel_id=1, source_target_pairs={{0,4},{2,6},{4,8},{6,10},{8,12},{10,14},{12,0},{14,2},{1,5},{3,7},... | collective-permute-start | bytes 884744 | tf_op jit(solution)/shard_map/ppermute | solution.py:256
  95.2 18.4 %collective-permute-start.13 = (bf16[144,1024]{1,0:T(8,128)(2,1)S(1)}, bf16[144,1024]{1,0:T(8,128)(2,1)S(1)}, u32[]{:S(2)}, u32[]{:S(2)}) collective-permute-start(bf16[144,1024]{1,0:T(8,128)(2,1)S(1)} %get-tuple-element.27), channel_id=1, source_target_pairs={{0,12},{2,14},{4,0},{6,2},{8,4},{10,6},{12,8},{14,10},{1,13},{3,15... | collective-permute-start | bytes 884744 | tf_op jit(solution)/shard_map/ppermute | solution.py:256
  98.5 17.3 %collective-permute-start.9 = (bf16[96,1024]{1,0:T(8,128)(2,1)S(1)}, bf16[96,1024]{1,0:T(8,128)(2,1)S(1)}, u32[]{:S(2)}, u32[]{:S(2)}) collective-permute-start(bf16[96,1024]{1,0:T(8,128)(2,1)S(1)} %get-tuple-element.24), channel_id=1, source_target_pairs={{0,2},{2,4},{4,6},{6,8},{8,10},{10,12},{12,14},{14,0},{1,3},{3,5},... | collective-permute-start | bytes 589832 | tf_op jit(solution)/shard_map/ppermute | solution.py:256
  99.1 30.2 %collective-permute-start.11 = (bf16[96,1024]{1,0:T(8,128)(2,1)S(1)}, bf16[96,1024]{1,0:T(8,128)(2,1)S(1)}, u32[]{:S(2)}, u32[]{:S(2)}) collective-permute-start(bf16[96,1024]{1,0:T(8,128)(2,1)S(1)} %get-tuple-element.26), channel_id=1, source_target_pairs={{0,6},{2,8},{4,10},{6,12},{8,14},{10,0},{12,2},{14,4},{1,7},{3,9},... | collective-permute-start | bytes 589832 | tf_op jit(solution)/shard_map/ppermute | solution.py:256
  108.7 20.6 %collective-permute-start.15 = (bf16[96,1024]{1,0:T(8,128)(2,1)S(1)}, bf16[96,1024]{1,0:T(8,128)(2,1)S(1)}, u32[]{:S(2)}, u32[]{:S(2)}) collective-permute-start(bf16[96,1024]{1,0:T(8,128)(2,1)S(1)} %get-tuple-element.28), channel_id=1, source_target_pairs={{0,10},{2,12},{4,14},{6,0},{8,2},{10,4},{12,6},{14,8},{1,11},{3,13... | collective-permute-start | bytes 589832 | tf_op jit(solution)/shard_map/ppermute | solution.py:256
  113.6 16.2 %collective-permute-start.16 = (bf16[96,1024]{1,0:T(8,128)(2,1)S(1)}, bf16[96,1024]{1,0:T(8,128)(2,1)S(1)}, u32[]{:S(2)}, u32[]{:S(2)}) collective-permute-start(bf16[96,1024]{1,0:T(8,128)(2,1)S(1)} %get-tuple-element.29), channel_id=1, source_target_pairs={{0,14},{2,0},{4,2},{6,4},{8,6},{10,8},{12,10},{14,12},{1,15},{3,1}... | collective-permute-start | bytes 589832 | tf_op jit(solution)/shard_map/ppermute | solution.py:256
  115.8 15.8 %collective-permute-start.12 = (bf16[48,1024]{1,0:T(8,128)(2,1)S(1)}, bf16[48,1024]{1,0:T(8,128)(2,1)S(1)}, u32[]{:S(2)}, u32[]{:S(2)}) collective-permute-start(bf16[48,1024]{1,0:T(8,128)(2,1)S(1)} %slice.34), channel_id=1, source_target_pairs={{0,4},{2,6},{4,8},{6,10},{8,12},{10,14},{12,0},{14,2},{1,5},{3,7},... | collective-permute-start | bytes 294920 | tf_op jit(solution)/shard_map/ppermute | solution.py:256
  129.3 4.8 %collective-permute-start.14 = (bf16[48,1024]{1,0:T(8,128)(2,1)S(1)}, bf16[48,1024]{1,0:T(8,128)(2,1)S(1)}, u32[]{:S(2)}, u32[]{:S(2)}) collective-permute-start(bf16[48,1024]{1,0:T(8,128)(2,1)S(1)} %slice.35), channel_id=1, source_target_pairs={{0,12},{2,14},{4,0},{6,2},{8,4},{10,6},{12,8},{14,10},{1,13},{3,15... | collective-permute-start | bytes 294920 | tf_op jit(solution)/shard_map/ppermute | solution.py:256
  138.5 2.0 %copy-start.3 = (bf16[1,1792,1024]{2,1,0:T(8,128)(2,1)S(1)}, bf16[1,1792,1024]{2,1,0:T(8,128)(2,1)}, u32[]{:S(2)}) copy-start(bf16[1,1792,1024]{2,1,0:T(8,128)(2,1)} %param.11) | copy-start | bytes 11010052
  140.6 2.0 %copy-start.5 = (bf16[1792,1024]{1,0:T(8,128)(2,1)S(1)}, bf16[1792,1024]{1,0:T(8,128)(2,1)}, u32[]{:S(2)}) copy-start(bf16[1792,1024]{1,0:T(8,128)(2,1)} %copy-done.4) | copy-start | bytes 11010052
  159.9 15.0 %collective-permute-start.18 = (bf16[1792,1024]{1,0:T(8,128)(2,1)}, bf16[1792,1024]{1,0:T(8,128)(2,1)}, u32[]{:S(2)}, u32[]{:S(2)}) collective-permute-start(bf16[1792,1024]{1,0:T(8,128)(2,1)} %convolution_convert_fusion), channel_id=1, source_target_pairs={{0,1},{1,0},{2,3},{3,2},{4,5},{5,4},{6,7},{7,6},{8,9},{9,8},{10,11... | collective-permute-start | bytes 11010056 | tf_op jit(solution)/shard_map/ppermute | solution.py:519
  161.7 23.9 %all-to-all-start.2 = ((f32[128,1,6]{2,1,0:T(1,128)}), f32[128,1,6]{2,1,0:T(1,128)S(1)}, u32[]{:S(2)}, u32[]{:S(2)}) async-start(f32[128,1,6]{2,1,0:T(1,128)} %bitcast.11), calls=%async_computation.2 | async-start | bytes 131072 | tf_op jit(solution)/shard_map/all_to_all | solution.py:509
  (5 other events, 7.1 us)
